TPU v7x, 128 devices: a whole 4x4x4 slice. The times are simulated.
128 devices in a mesh: by: 8 (over x_hi, z), bx: 16 (over x_lo, y, core).
Axes of the slice: x: 4 (x_hi: 2, x_lo: 2; x = x_hi * 2 + x_lo), y: 4, z: 4, core: 2. Of those that a mesh axis runs over, the one named last changes fastest.
Arguments:
- eastward_flow: float32 [62, 64, 4096], P(None, 'by', 'bx'), may hold values from -6 to 6
- northward_flow: float32 [62, 64, 4096], P(None, 'by', 'bx'), may hold values from -6 to 6
- heat_anomaly: float32 [62, 64, 4096], P(None, 'by', 'bx'), may hold values from -6 to 6
- salt_anomaly: float32 [62, 64, 4096], P(None, 'by', 'bx'), may hold values from -6 to 6
- air_stress_forcing: float32 [2, 64, 4096], P(None, 'by', 'bx'), may hold values from -6 to 6
- earlier_sea_height_load: float32 [64, 4096], P('by', 'bx'), may hold values from -6 to 6
- ocean_layer_depths: int32 [64, 4096], P('by', 'bx'), may hold values from 0 to 62, as said below
Outputs:
- east_new: float32 [62, 64, 4096], P(None, 'by', 'bx')
- north_new: float32 [62, 64, 4096], P(None, 'by', 'bx')
- temperature_new: float32 [62, 64, 4096], P(None, 'by', 'bx')
- salinity_new: float32 [62, 64, 4096], P(None, 'by', 'bx')
- surface_new: float32 [64, 4096], P('by', 'bx')
Inputs may be any that keep to these rules, and one draw needn't show every extreme that they name: `ocean_layer_depths`: land (0) covers whole aligned tiles of 8 x 8 cells; every ocean column has 1 to 62 levels.
All inputs are finite; a program needn't handle non-finite values.
Results may differ from a plain program's by a relative error of at most 0.0003.
Values sent between devices are 32-bit elements; how exact they have to be, the bound alone decides.
A program may use at most 192 MiB of HBM per device.

v0:
```python
import math

import jax
import jax.numpy as jnp
from jax import lax
from jax.sharding import PartitionSpec as P

ITERS = 4


KAPPA = 0.004
ADVECT = 0.25
PRESS = 0.1
WIND = 0.5
PHI = 0.5
DIVERGE = 2.0
LOWER = 0.2
UPPER = 2.0


def extended(cells, sides, width):
    for axis, dim in sides:
        count = lax.axis_size(axis)
        head = lax.slice_in_dim(cells, 0, width, axis=dim)
        tail = lax.slice_in_dim(cells, cells.shape[dim] - width, cells.shape[dim], axis=dim)
        cells = jnp.concatenate(
            [
                lax.ppermute(tail, axis, [(i, (i + 1) % count) for i in range(count)]),
                cells,
                lax.ppermute(head, axis, [((i + 1) % count, i) for i in range(count)]),
            ],
            axis=dim,
        )
    return cells


def chebyshev_weights(count):
    middle = 0.5 * (UPPER + LOWER)
    half_span = 0.5 * (UPPER - LOWER)
    ratio_value = middle / half_span
    rho_now = 1.0 / ratio_value
    updates = []
    for index in range(count - 1):
        rho_next = 1.0 / (2.0 * ratio_value - rho_now)
        updates.append((rho_next * rho_now, 2.0 * rho_next / half_span))
        rho_now = rho_next
    return (1.0 / middle, updates)


def shrink(field, width):
    return field[..., width : field.shape[-2] - width, width : field.shape[-1] - width]


def sides(field):
    return (
        field[..., 1:-1, 1:-1],
        field[..., 1:-1, 2:],
        field[..., 1:-1, :-2],
        field[..., 2:, 1:-1],
        field[..., :-2, 1:-1],
    )


def laplacian(field, mask):
    cell_here, cell_east, cell_west, cell_north, cell_south = sides(field)
    mask_here, mask_east, mask_west, mask_north, mask_south = sides(mask)
    return (
        mask_here * mask_east * (cell_east - cell_here)
        + mask_here * mask_west * (cell_west - cell_here)
        + mask_here * mask_north * (cell_north - cell_here)
        + mask_here * mask_south * (cell_south - cell_here)
    )


def gradients(field, mask):
    cell_here, cell_east, cell_west, cell_north, cell_south = sides(field)
    mask_here, mask_east, mask_west, mask_north, mask_south = sides(mask)
    along_x = 0.5 * (
        mask_here * mask_east * (cell_east - cell_here)
        + mask_here * mask_west * (cell_here - cell_west)
    )
    along_y = 0.5 * (
        mask_here * mask_north * (cell_north - cell_here)
        + mask_here * mask_south * (cell_here - cell_south)
    )
    return (along_x, along_y)


def wet_levels(depth, levels):
    return jnp.where(jnp.arange(levels)[:, None, None] < depth[None], 1.0, 0.0).astype(jnp.float32)


def coriolis_rows(first_row, count, total_rows):
    rows_float = (first_row + jnp.arange(count)).astype(jnp.float32)
    return (1.2 * jnp.sin(0.9 * math.pi * ((rows_float + 0.5) / total_rows - 0.5)))[:, None]


def tendency(ocean_state_arrays, wind, wet, coriolis):
    east_vel, north_vel, temper, saline = ocean_state_arrays
    inner = shrink(wet, 2)
    rotate = coriolis[2 : coriolis.shape[0] - 2]
    density = (-0.8 * temper + 0.6 * saline) * wet
    pressure = PRESS * jnp.cumsum(density, axis=0)
    press_x, press_y = gradients(pressure, wet)
    press_x = shrink(press_x, 1)
    press_y = shrink(press_y, 1)
    east_in = shrink(east_vel, 2)
    north_in = shrink(north_vel, 2)
    inner_mask = shrink(wet, 1)

    def mixing(field):
        slope_x, slope_y = gradients(field, wet)
        carried = east_in * shrink(slope_x, 1) + north_in * shrink(slope_y, 1)
        smoothed = laplacian(laplacian(field, wet), inner_mask)
        return -ADVECT * carried - KAPPA * smoothed

    east_tend = inner * (rotate * north_in - press_x + mixing(east_vel))
    north_tend = inner * (-rotate * east_in - press_y + mixing(north_vel))
    east_top = east_tend[:1] + WIND * inner[:1] * shrink(wind[0:1], 2)
    north_top = north_tend[:1] + WIND * inner[:1] * shrink(wind[1:2], 2)
    east_tend = jnp.concatenate([east_top, east_tend[1:]], axis=0)
    north_tend = jnp.concatenate([north_top, north_tend[1:]], axis=0)
    return (east_tend, north_tend, inner * mixing(temper), inner * mixing(saline))


def corner_depth(depth, levels):
    smallest = jnp.minimum(
        jnp.minimum(depth[:-1, :-1], depth[:-1, 1:]), jnp.minimum(depth[1:, :-1], depth[1:, 1:])
    )
    return smallest.astype(jnp.float32) / levels


def diagonal_of(depth):
    return PHI + 0.5 * (depth[1:, 1:] + depth[1:, :-1] + depth[:-1, 1:] + depth[:-1, :-1])


def apply_operator(field, depth):
    low_left = field[:-1, :-1]
    low_right = field[:-1, 1:]
    up_left = field[1:, :-1]
    up_right = field[1:, 1:]
    slope_x = 0.5 * (low_right + up_right - low_left - up_left)
    slope_y = 0.5 * (up_left + up_right - low_left - low_right)
    flux_x = depth * slope_x
    flux_y = depth * slope_y
    spread = 0.5 * (
        flux_x[1:, 1:]
        + flux_x[:-1, 1:]
        - (flux_x[1:, :-1] + flux_x[:-1, :-1])
        + (flux_y[1:, 1:] + flux_y[1:, :-1])
        - (flux_y[:-1, 1:] + flux_y[:-1, :-1])
    )
    return PHI * field[1:-1, 1:-1] - spread


def region(field, width):
    return field[4 - width : field.shape[0] - 4 + width, 4 - width : field.shape[1] - 4 + width]


def outer_region(field, width, margin):
    return field[
        margin - width : field.shape[0] - margin + width,
        margin - width : field.shape[1] - margin + width,
    ]


def state_rims(ocean_state_arrays):
    return (
        extended(ocean_state_arrays[0], (("by", 1), ("bx", 2)), 2),
        extended(ocean_state_arrays[1], (("by", 1), ("bx", 2)), 2),
        extended(ocean_state_arrays[2], (("by", 1), ("bx", 2)), 2),
        extended(ocean_state_arrays[3], (("by", 1), ("bx", 2)), 2),
    )


def body(
    eastward_flow,
    northward_flow,
    heat_anomaly,
    salt_anomaly,
    air_stress_forcing,
    earlier_sea_height_load,
    ocean_layer_depths,
):
    rows, columns = earlier_sea_height_load.shape
    levels = eastward_flow.shape[0]
    total_rows = rows * lax.axis_size("by")
    first_row = lax.axis_index("by") * rows
    margin = max(4, ITERS + 1)
    depth_halo = extended(ocean_layer_depths, (("by", 0), ("bx", 1)), margin)
    row_index = first_row - margin + jnp.arange(rows + 2 * margin)
    inside = (row_index >= 0) & (row_index < total_rows)
    depth_big = jnp.where(inside[:, None], depth_halo, 0)
    depth_pad = outer_region(depth_big, 4, margin)
    ocean_state_arrays = (eastward_flow, northward_flow, heat_anomaly, salt_anomaly)
    wet_two = wet_levels(region(depth_pad, 2), levels)
    coriolis = coriolis_rows(first_row - 2, rows + 4, total_rows)
    wind_pad = jnp.pad(air_stress_forcing, ((0, 0), (2, 2), (2, 2)))
    first = tendency(state_rims(ocean_state_arrays), wind_pad, wet_two, coriolis)
    provisional = tuple((item + extra for item, extra in zip(ocean_state_arrays, first)))
    second = tendency(state_rims(provisional), wind_pad, wet_two, coriolis)
    wet_in = shrink(wet_two, 2)
    updated = tuple(
        (
            item + 0.5 * (term_first + term_second)
            for item, term_first, term_second in zip(ocean_state_arrays, first, second)
        )
    )
    transport_east = jnp.sum(wet_in * updated[0], axis=0) / levels
    transport_north = jnp.sum(wet_in * updated[1], axis=0) / levels
    opening, updates = chebyshev_weights(ITERS)
    east_pad, north_pad, surface_pad = (
        extended(transport_east, (("by", 0), ("bx", 1)), 1),
        extended(transport_north, (("by", 0), ("bx", 1)), 1),
        extended(earlier_sea_height_load, (("by", 0), ("bx", 1)), 1),
    )
    column_one = jnp.where(region(depth_pad, 1) > 0, 1.0, 0.0).astype(jnp.float32)
    slope_x = gradients(east_pad, column_one)[0]
    slope_y = gradients(north_pad, column_one)[1]
    forcing = shrink(column_one, 1) * (
        PHI * earlier_sea_height_load - DIVERGE * (slope_x + slope_y)
    )
    depth_one = corner_depth(region(depth_pad, 1), levels)
    diagonal = diagonal_of(depth_one)
    residual = forcing - apply_operator(surface_pad, depth_one)
    direction = opening * (residual / diagonal)
    solution = earlier_sea_height_load
    for index in range(ITERS):
        solution = solution + direction
        if index + 1 < ITERS:
            direction_pad = extended(direction, (("by", 0), ("bx", 1)), 1)
            residual = residual - apply_operator(direction_pad, depth_one)
            keep, push = updates[index]
            direction = keep * direction + push * (residual / diagonal)
    return (updated[0], updated[1], updated[2], updated[3], solution)


def solution(mesh):
    return jax.shard_map(
        body,
        mesh=mesh,
        in_specs=(
            P(None, "by", "bx"),
            P(None, "by", "bx"),
            P(None, "by", "bx"),
            P(None, "by", "bx"),
            P(None, "by", "bx"),
            P("by", "bx"),
            P("by", "bx"),
        ),
        out_specs=(
            P(None, "by", "bx"),
            P(None, "by", "bx"),
            P(None, "by", "bx"),
            P(None, "by", "bx"),
            P("by", "bx"),
        ),
        check_vma=False,
    )
```

profile of v0, /device:TPU:6, one launch (start us, length us, event | category | flops | bytes accessed | tf_op | source)
XLA Modules:
  0.0 321.9 jit_solution(6699360753356391404)
XLA Ops:
  4.1 3.7 %collective-permute-start.5 = (f32[62,2,256]{2,1,0:T(2,128)S(1)}, f32[62,2,256]{2,1,0:T(2,128)S(1)}, u32[]{:S(2)}, u32[]{:S(2)}) collective-permute-start(f32[62,2,256]{2,1,0:T(2,128)S(1)} %get-tuple-element.142), channel_id=1, source_target_pairs={{16,0},{32,16},{48,32},{64,48},{80,64},{96,80},{112,96},{0,112},{1... | collective-permute-start | bytes 380936 | tf_op jit(solution)/shard_map/ppermute | solution.py:30
  9.6 5.4 %collective-permute-start.43 = (f32[1,256]{1,0:T(1,128)S(1)}, f32[1,256]{1,0:T(1,128)S(1)}, u32[]{:S(2)}, u32[]{:S(2)}) collective-permute-start(f32[1,256]{1,0:T(1,128)S(1)} %get-tuple-element.180), channel_id=1, source_target_pairs={{16,0},{32,16},{48,32},{64,48},{80,64},{96,80},{112,96},{0,112},{1... | collective-permute-start | bytes 3080 | tf_op jit(solution)/shard_map/ppermute | solution.py:30
  23.4 3.4 %collective-permute-done.45 = f32[10,1]{1,0:T(8,128)S(1)} collective-permute-done((f32[10,1]{1,0:T(8,128)S(1)}, f32[10,1]{1,0:T(8,128)S(1)}, u32[]{:S(2)}, u32[]{:S(2)}) %collective-permute-start.45) | collective-permute-done | bytes 72 | tf_op jit(solution)/shard_map/ppermute | solution.py:28
  27.8 6.0 %collective-permute-start.13 = (f32[62,2,256]{2,1,0:T(2,128)S(1)}, f32[62,2,256]{2,1,0:T(2,128)S(1)}, u32[]{:S(2)}, u32[]{:S(2)}) collective-permute-start(f32[62,2,256]{2,1,0:T(2,128)S(1)} %get-tuple-element.134), channel_id=1, source_target_pairs={{16,0},{32,16},{48,32},{64,48},{80,64},{96,80},{112,96},{0,112},{1... | collective-permute-start | bytes 380936 | tf_op jit(solution)/shard_map/ppermute | solution.py:30
  36.0 5.7 %collective-permute-start.9 = (f32[62,2,256]{2,1,0:T(2,128)S(1)}, f32[62,2,256]{2,1,0:T(2,128)S(1)}, u32[]{:S(2)}, u32[]{:S(2)}) collective-permute-start(f32[62,2,256]{2,1,0:T(2,128)S(1)} %get-tuple-element.140), channel_id=1, source_target_pairs={{16,0},{32,16},{48,32},{64,48},{80,64},{96,80},{112,96},{0,112},{1... | collective-permute-start | bytes 380936 | tf_op jit(solution)/shard_map/ppermute | solution.py:30
  42.2 5.7 %collective-permute-start.17 = (f32[62,2,256]{2,1,0:T(2,128)S(1)}, f32[62,2,256]{2,1,0:T(2,128)S(1)}, u32[]{:S(2)}, u32[]{:S(2)}) collective-permute-start(f32[62,2,256]{2,1,0:T(2,128)S(1)} %get-tuple-element.136), channel_id=1, source_target_pairs={{16,0},{32,16},{48,32},{64,48},{80,64},{96,80},{112,96},{0,112},{1... | collective-permute-start | bytes 380936 | tf_op jit(solution)/shard_map/ppermute | solution.py:30
  48.3 3.9 %collective-permute-start.7 = (f32[62,12,2]{2,1,0:T(8,128)S(1)}, f32[62,12,2]{2,1,0:T(8,128)S(1)}, u32[]{:S(2)}, u32[]{:S(2)}) collective-permute-start(f32[62,12,2]{2,1,0:T(8,128)S(1)} %get-tuple-element.126), channel_id=1, source_target_pairs={{1,0},{2,1},{3,2},{4,3},{5,4},{6,5},{7,6},{8,7},{9,8},{10,9},{11,1... | collective-permute-start | bytes 17864 | tf_op jit(solution)/shard_map/ppermute | solution.py:30
  52.6 3.9 %collective-permute-start.14 = (f32[62,12,2]{2,1,0:T(8,128)S(1)}, f32[62,12,2]{2,1,0:T(8,128)S(1)}, u32[]{:S(2)}, u32[]{:S(2)}) collective-permute-start(f32[62,12,2]{2,1,0:T(8,128)S(1)} %get-tuple-element.118), channel_id=1, source_target_pairs={{1,0},{2,1},{3,2},{4,3},{5,4},{6,5},{7,6},{8,7},{9,8},{10,9},{11,1... | collective-permute-start | bytes 17864 | tf_op jit(solution)/shard_map/ppermute | solution.py:30
  58.4 3.4 %collective-permute-start.11 = (f32[62,12,2]{2,1,0:T(8,128)S(1)}, f32[62,12,2]{2,1,0:T(8,128)S(1)}, u32[]{:S(2)}, u32[]{:S(2)}) collective-permute-start(f32[62,12,2]{2,1,0:T(8,128)S(1)} %get-tuple-element.124), channel_id=1, source_target_pairs={{1,0},{2,1},{3,2},{4,3},{5,4},{6,5},{7,6},{8,7},{9,8},{10,9},{11,1... | collective-permute-start | bytes 17864 | tf_op jit(solution)/shard_map/ppermute | solution.py:30
  63.1 6.1 %collective-permute-done.10 = f32[62,12,2]{2,1,0:T(8,128)S(1)} collective-permute-done((f32[62,12,2]{2,1,0:T(8,128)S(1)}, f32[62,12,2]{2,1,0:T(8,128)S(1)}, u32[]{:S(2)}, u32[]{:S(2)}) %collective-permute-start.10) | collective-permute-done | bytes 5984 | tf_op jit(solution)/shard_map/ppermute | solution.py:28
  71.8 6.0 %fusion.318 = (f32[62,10,258]{2,1,0:T(8,128)}, f32[62,10,258]{2,1,0:T(8,128)}, f32[62,10,258]{2,1,0:T(8,128)}, f32[62,10,258]{2,1,0:T(8,128)S(1)}, f32[62,10,258...) fusion(f32[62,12,260]{2,1,0:T(8,128)S(1)} %pad_maximum_fusion.4, ...), kind=kLoop, calls=%fused_computation.526 | loop fusion | flops 3359160 | bytes 11651040 | tf_op jit(solution)/shard_map/slice | solution.py:56
  82.8 4.9 %fusion.321 = (f32[62,10,258]{2,1,0:T(8,128)S(1)}, f32[62,10,258]{2,1,0:T(8,128)}, f32[62,10,258]{2,1,0:T(8,128)S(1)}, f32[62,10,258]{2,1,0:T(8,128)}, f32[62,10,258]{2,1,0:T(8,128)}) fusion(f32[62,12,260]{2,1,0:T(8,128)S(1)} %pad_maximum_fusion.50, f32[62,10,258]{2,1,0:T(8,128)S(1)} %get-tuple-element.75, f32[62,10,258]{2,1,0:T(8,128)S(1)} %get-tuple-element.77, ...), kind=kLoop, calls=%fused_computation.529 | loop fusion | flops 2719320 | bytes 8451840 | tf_op jit(solution)/shard_map/slice | solution.py:56
  87.7 4.9 %fusion.206 = f32[62,8,256]{2,1,0:T(8,128)S(1)} fusion(f32[62,10,258]{2,1,0:T(8,128)S(1)} %get-tuple-element.93, f32[62,8,256]{2,1,0:T(8,128)S(1)} %copy-done.9, f32[62,10,258]{2,1,0:T(8,128)} %get-tuple-element.94, f32[62,10,258]{2,1,0:T(8,128)} %get-tuple-element.92, f32[62,8,256]{2,1,0:T(8,128)S(1)} %copy-done.10, f32[62,10,258]{2,1,0:T(8,128)} %get-tuple-element.95, ...), kind=kLoop, calls=%fused_computation.350 | loop fusion | flops 4952064 | bytes 12189728 | tf_op jit(solution)/shard_map/mul | solution.py:117
  97.9 13.2 %fusion.322 = (f32[62,10,258]{2,1,0:T(8,128)S(1)}, f32[62,10,258]{2,1,0:T(8,128)S(1)}, f32[62,10,258]{2,1,0:T(8,128)S(1)}, f32[62,10,258]{2,1,0:T(8,128)S(1)}, f32[62,10,258]{2,1,0:T(8,128)}) fusion(f32[62,12,260]{2,1,0:T(8,128)S(1)} %pad_maximum_fusion.51, f32[62,10,258]{2,1,0:T(8,128)S(1)} %get-tuple-element.75, f32[62,10,258]{2,1,0:T(8,128)S(1)} %get-tuple-element.77, ...), kind=kLoop, calls=%fused_computation.530 | loop fusion | flops 2719320 | bytes 8451840 | tf_op jit(solution)/shard_map/slice | solution.py:56
  111.1 4.5 %fusion.182 = f32[62,8,256]{2,1,0:T(8,128)S(1)} fusion(f32[62,10,258]{2,1,0:T(8,128)S(1)} %get-tuple-element.98, f32[62,8,256]{2,1,0:T(8,128)S(1)} %copy-done.9, f32[62,10,258]{2,1,0:T(8,128)S(1)} %get-tuple-element.99, f32[62,10,258]{2,1,0:T(8,128)S(1)} %get-tuple-element.97, f32[62,8,256]{2,1,0:T(8,128)S(1)} %copy-done.10, ...), kind=kLoop, calls=%fused_computation.316 | loop fusion | flops 4952064 | bytes 12189728 | tf_op jit(solution)/shard_map/mul | solution.py:118
  116.5 4.4 %fusion.324 = (f32[62,10,258]{2,1,0:T(8,128)}, f32[62,10,258]{2,1,0:T(8,128)}, f32[62,10,258]{2,1,0:T(8,128)}, f32[62,10,258]{2,1,0:T(8,128)}, f32[62,10,258]{2,1,0:T(8,128)}) fusion(f32[62,12,260]{2,1,0:T(8,128)S(1)} %pad_maximum_fusion.49, f32[62,10,258]{2,1,0:T(8,128)S(1)} %get-tuple-element.75, f32[62,10,258]{2,1,0:T(8,128)S(1)} %get-tuple-element.77, ...), kind=kLoop, calls=%fused_computation.532 | loop fusion | flops 2719320 | bytes 8451840 | tf_op jit(solution)/shard_map/slice | solution.py:56
  123.1 9.3 %fusion.305 = (f32[62,8,256]{2,1,0:T(8,128)}, f32[62,8,256]{2,1,0:T(8,128)}) fusion(f32[62,8,256]{2,1,0:T(8,128)} %param.10, f32[62,10,258]{2,1,0:T(8,128)} %get-tuple-element.108, f32[62,12,260]{2,1,0:T(8,128)S(1)} %fusion.34, f32[62,8,256]{2,1,0:T(8,128)S(1)} %copy-done.9, f32[62,10,258]{2,1,0:T(8,128)} %get-tuple-element.107, ...), kind=kLoop, calls=%fused_computation.522 | loop fusion | flops 3936256 | bytes 11173888 | tf_op jit(solution)/shard_map/add | solution.py:200
  134.5 5.6 %collective-permute-start.25 = (f32[62,2,256]{2,1,0:T(2,128)}, f32[62,2,256]{2,1,0:T(2,128)}, u32[]{:S(2)}, u32[]{:S(2)}) collective-permute-start(f32[62,2,256]{2,1,0:T(2,128)} %get-tuple-element.138), channel_id=1, source_target_pairs={{16,0},{32,16},{48,32},{64,48},{80,64},{96,80},{112,96},{0,112},{1... | collective-permute-start | bytes 380936 | tf_op jit(solution)/shard_map/ppermute | solution.py:30
  140.1 3.4 %pad_maximum_fusion.30 = f32[62,10,258]{2,1,0:T(8,128)} fusion(f32[62,12,2]{2,1,0:T(8,128)} %copy-done.23, f32[62,2,256]{2,1,0:T(2,128)} %copy-done.34, f32[62,8,256]{2,1,0:T(8,128)} %param.9, f32[62,2,256]{2,1,0:T(2,128)} %copy-done.32), kind=kLoop, calls=%fused_computation.52 | loop fusion | flops 479880 | bytes 1407648 | tf_op jit(solution)/shard_map/concatenate | solution.py:26
  143.6 9.2 %fusion.301 = (f32[62,8,256]{2,1,0:T(8,128)}, f32[62,8,256]{2,1,0:T(8,128)}) fusion(f32[62,8,256]{2,1,0:T(8,128)} %param.9, f32[62,10,258]{2,1,0:T(8,128)} %get-tuple-element.74, f32[62,12,260]{2,1,0:T(8,128)S(1)} %fusion.34, f32[62,8,256]{2,1,0:T(8,128)S(1)} %copy-done.9, f32[62,10,258]{2,1,0:T(8,128)} %get-tuple-element.73, ...), kind=kLoop, calls=%fused_computation.521 | loop fusion | flops 3936256 | bytes 11173888 | tf_op jit(solution)/shard_map/add | solution.py:200
  154.3 5.6 %collective-permute-start.21 = (f32[62,2,256]{2,1,0:T(2,128)S(1)}, f32[62,2,256]{2,1,0:T(2,128)S(1)}, u32[]{:S(2)}, u32[]{:S(2)}) collective-permute-start(f32[62,2,256]{2,1,0:T(2,128)S(1)} %get-tuple-element.130), channel_id=1, source_target_pairs={{16,0},{32,16},{48,32},{64,48},{80,64},{96,80},{112,96},{0,112},{1... | collective-permute-start | bytes 380936 | tf_op jit(solution)/shard_map/ppermute | solution.py:30
  163.1 3.8 %collective-permute-start.27 = (f32[62,12,2]{2,1,0:T(8,128)S(1)}, f32[62,12,2]{2,1,0:T(8,128)S(1)}, u32[]{:S(2)}, u32[]{:S(2)}) collective-permute-start(f32[62,12,2]{2,1,0:T(8,128)S(1)} %get-tuple-element.122), channel_id=1, source_target_pairs={{1,0},{2,1},{3,2},{4,3},{5,4},{6,5},{7,6},{8,7},{9,8},{10,9},{11,1... | collective-permute-start | bytes 17864 | tf_op jit(solution)/shard_map/ppermute | solution.py:30
  168.2 3.8 %collective-permute-start.23 = (f32[62,12,2]{2,1,0:T(8,128)}, f32[62,12,2]{2,1,0:T(8,128)}, u32[]{:S(2)}, u32[]{:S(2)}) collective-permute-start(f32[62,12,2]{2,1,0:T(8,128)} %get-tuple-element.114), channel_id=1, source_target_pairs={{1,0},{2,1},{3,2},{4,3},{5,4},{6,5},{7,6},{8,7},{9,8},{10,9},{11,1... | collective-permute-start | bytes 17864 | tf_op jit(solution)/shard_map/ppermute | solution.py:30
  173.6 3.3 %pad_maximum_fusion = f32[62,10,258]{2,1,0:T(8,128)} fusion(f32[62,12,2]{2,1,0:T(8,128)S(1)} %collective-permute-done.26, f32[62,2,256]{2,1,0:T(2,128)} %collective-permute-done.25, f32[62,8,256]{2,1,0:T(8,128)S(1)} %copy-done.22, f32[62,2,256]{2,1,0:T(2,128)} %collective-permute-done.24), kind=kLoop, calls=%fused_computation.2 | loop fusion | flops 479880 | bytes 1407648 | tf_op jit(solution)/shard_map/concatenate | solution.py:26
  179.2 5.6 %fusion.323 = (f32[62,10,258]{2,1,0:T(8,128)}, f32[62,10,258]{2,1,0:T(8,128)}, f32[62,10,258]{2,1,0:T(8,128)}, f32[62,10,258]{2,1,0:T(8,128)}, f32[62,10,258]{2,1,0:T(8,128)}) fusion(f32[62,12,260]{2,1,0:T(8,128)S(1)} %pad_maximum_fusion.53, f32[62,10,258]{2,1,0:T(8,128)S(1)} %get-tuple-element.75, f32[62,10,258]{2,1,0:T(8,128)S(1)} %copy-done.4, ...), kind=kLoop, calls=%fused_computation.531 | loop fusion | flops 2719320 | bytes 8451840 | tf_op jit(solution)/shard_map/slice | solution.py:56
  184.8 9.5 %fusion.58 = (f32[62,8,256]{2,1,0:T(8,128)}, f32[62,8,256]{2,1,0:T(8,128)}, f32[62,8,256]{2,1,0:T(8,128)}) fusion(f32[62,8,256]{2,1,0:T(8,128)} %param.10, f32[62,8,256]{2,1,0:T(8,128)} %get-tuple-element.40, f32[62,10,258]{2,1,0:T(8,128)} %get-tuple-element.103, f32[62,10,258]{2,1,0:T(8,128)} %get-tuple-element.104, f32[62,10,258]{2,1,0:T(8,128)} %get-tuple-element.102, ...), kind=kLoop, calls=%fused_computation.140 | loop fusion | flops 4698112 | bytes 13205504 | tf_op jit(solution)/shard_map/add | solution.py:205
  195.7 6.0 %collective-permute-start.29 = (f32[62,2,256]{2,1,0:T(2,128)S(1)}, f32[62,2,256]{2,1,0:T(2,128)S(1)}, u32[]{:S(2)}, u32[]{:S(2)}) collective-permute-start(f32[62,2,256]{2,1,0:T(2,128)S(1)} %get-tuple-element.128), channel_id=1, source_target_pairs={{16,0},{32,16},{48,32},{64,48},{80,64},{96,80},{112,96},{0,112},{1... | collective-permute-start | bytes 380936 | tf_op jit(solution)/shard_map/ppermute | solution.py:30
  201.7 2.5 pad_maximum_fusion.52
  206.6 5.6 %collective-permute-start.33 = (f32[62,2,256]{2,1,0:T(2,128)S(1)}, f32[62,2,256]{2,1,0:T(2,128)S(1)}, u32[]{:S(2)}, u32[]{:S(2)}) collective-permute-start(f32[62,2,256]{2,1,0:T(2,128)S(1)} %get-tuple-element.132), channel_id=1, source_target_pairs={{16,0},{32,16},{48,32},{64,48},{80,64},{96,80},{112,96},{0,112},{1... | collective-permute-start | bytes 380936 | tf_op jit(solution)/shard_map/ppermute | solution.py:30
  212.7 3.8 %collective-permute-start.30 = (f32[62,12,2]{2,1,0:T(8,128)S(1)}, f32[62,12,2]{2,1,0:T(8,128)S(1)}, u32[]{:S(2)}, u32[]{:S(2)}) collective-permute-start(f32[62,12,2]{2,1,0:T(8,128)S(1)} %get-tuple-element.112), channel_id=1, source_target_pairs={{1,0},{2,1},{3,2},{4,3},{5,4},{6,5},{7,6},{8,7},{9,8},{10,9},{11,1... | collective-permute-start | bytes 17864 | tf_op jit(solution)/shard_map/ppermute | solution.py:30
  217.8 4.0 %collective-permute-start.34 = (f32[62,12,2]{2,1,0:T(8,128)}, f32[62,12,2]{2,1,0:T(8,128)S(1)}, u32[]{:S(2)}, u32[]{:S(2)}) collective-permute-start(f32[62,12,2]{2,1,0:T(8,128)} %get-tuple-element.116), channel_id=1, source_target_pairs={{1,0},{2,1},{3,2},{4,3},{5,4},{6,5},{7,6},{8,7},{9,8},{10,9},{11,1... | collective-permute-start | bytes 17864 | tf_op jit(solution)/shard_map/ppermute | solution.py:30
  223.2 2.3 pad_maximum_fusion.18
  227.4 3.9 %fusion.317 = (f32[62,10,258]{2,1,0:T(8,128)S(1)}, f32[62,10,258]{2,1,0:T(8,128)}, f32[62,10,258]{2,1,0:T(8,128)S(1)}, f32[62,10,258]{2,1,0:T(8,128)}, f32[62,10,258]{2,1,0:T(8,128)}) fusion(f32[62,12,260]{2,1,0:T(8,128)S(1)} %pad_maximum_fusion.54, f32[62,10,258]{2,1,0:T(8,128)S(1)} %get-tuple-element.75, f32[62,10,258]{2,1,0:T(8,128)S(1)} %copy-done.5, ...), kind=kLoop, calls=%fused_computation.525 | loop fusion | flops 2719320 | bytes 8451840 | tf_op jit(solution)/shard_map/slice | solution.py:56
  231.3 4.8 %fusion.122 = f32[62,8,256]{2,1,0:T(8,128)S(1)} fusion(f32[62,10,258]{2,1,0:T(8,128)S(1)} %get-tuple-element.69, f32[62,8,256]{2,1,0:T(8,128)S(1)} %copy-done.14, f32[62,10,258]{2,1,0:T(8,128)} %get-tuple-element.70, f32[62,10,258]{2,1,0:T(8,128)} %get-tuple-element.68, f32[62,8,256]{2,1,0:T(8,128)S(1)} %copy-done.16, f32[62,10,258]{2,1,0:T(8,128)} %get-tuple-element.71, ...), kind=kLoop, calls=%fused_computation.230 | loop fusion | flops 4952064 | bytes 12189728 | tf_op jit(solution)/shard_map/mul | solution.py:117
  240.3 3.4 %fusion.319 = (f32[62,10,258]{2,1,0:T(8,128)S(1)}, f32[62,10,258]{2,1,0:T(8,128)S(1)}, f32[62,10,258]{2,1,0:T(8,128)S(1)}, f32[62,10,258]{2,1,0:T(8,128)S(1)}, f32[62,10,258]{2,1,0:T(8,128)}) fusion(f32[62,12,260]{2,1,0:T(8,128)S(1)} %pad_maximum_fusion.55, f32[62,10,258]{2,1,0:T(8,128)S(1)} %get-tuple-element.75, f32[62,10,258]{2,1,0:T(8,128)S(1)} %copy-done.5, ...), kind=kLoop, calls=%fused_computation.527 | loop fusion | flops 2719320 | bytes 8451840 | tf_op jit(solution)/shard_map/slice | solution.py:56
  243.7 4.5 %fusion.98 = f32[62,8,256]{2,1,0:T(8,128)S(1)} fusion(f32[62,10,258]{2,1,0:T(8,128)S(1)} %get-tuple-element.83, f32[62,8,256]{2,1,0:T(8,128)S(1)} %copy-done.14, f32[62,10,258]{2,1,0:T(8,128)S(1)} %get-tuple-element.84, f32[62,10,258]{2,1,0:T(8,128)S(1)} %get-tuple-element.82, f32[62,8,256]{2,1,0:T(8,128)S(1)} %copy-done.16, ...), kind=kLoop, calls=%fused_computation.196 | loop fusion | flops 4952064 | bytes 12189728 | tf_op jit(solution)/shard_map/mul | solution.py:118
  248.5 2.4 multiply_reduce_fusion.1
  250.9 5.6 %collective-permute-start.37 = (f32[1,256]{1,0:T(1,128)S(1)}, f32[1,256]{1,0:T(1,128)S(1)}, u32[]{:S(2)}, u32[]{:S(2)}) collective-permute-start(f32[1,256]{1,0:T(1,128)S(1)} %get-tuple-element.176), channel_id=1, source_target_pairs={{16,0},{32,16},{48,32},{64,48},{80,64},{96,80},{112,96},{0,112},{1... | collective-permute-start | bytes 3080 | tf_op jit(solution)/shard_map/ppermute | solution.py:30
  260.1 3.7 %collective-permute-done.41 = f32[1,256]{1,0:T(1,128)S(1)} collective-permute-done((f32[1,256]{1,0:T(1,128)S(1)}, f32[1,256]{1,0:T(1,128)S(1)}, u32[]{:S(2)}, u32[]{:S(2)}) %collective-permute-start.41) | collective-permute-done | bytes 1056 | tf_op jit(solution)/shard_map/ppermute | solution.py:28
  264.4 5.6 %collective-permute-start.47 = (f32[1,256]{1,0:T(1,128)S(1)}, f32[1,256]{1,0:T(1,128)S(1)}, u32[]{:S(2)}, u32[]{:S(2)}) collective-permute-start(f32[1,256]{1,0:T(1,128)S(1)} %get-tuple-element.174), channel_id=1, source_target_pairs={{16,0},{32,16},{48,32},{64,48},{80,64},{96,80},{112,96},{0,112},{1... | collective-permute-start | bytes 3080 | tf_op jit(solution)/shard_map/ppermute | solution.py:30
  270.0 5.5 %fusion.315 = (f32[62,10,258]{2,1,0:T(8,128)}, f32[62,10,258]{2,1,0:T(8,128)}, f32[62,10,258]{2,1,0:T(8,128)}, f32[62,10,258]{2,1,0:T(8,128)}, f32[62,10,258]{2,1,0:T(8,128)}) fusion(f32[62,12,260]{2,1,0:T(8,128)S(1)} %pad_maximum_fusion.52, f32[62,10,258]{2,1,0:T(8,128)S(1)} %get-tuple-element.75, f32[62,10,258]{2,1,0:T(8,128)S(1)} %copy-done.5, ...), kind=kLoop, calls=%fused_computation.523 | loop fusion | flops 2719320 | bytes 8451840 | tf_op jit(solution)/shard_map/slice | solution.py:56
  277.0 3.9 %collective-permute-done.49 = f32[10,1]{1,0:T(8,128)S(1)} collective-permute-done((f32[10,1]{1,0:T(8,128)S(1)}, f32[10,1]{1,0:T(8,128)S(1)}, u32[]{:S(2)}, u32[]{:S(2)}) %collective-permute-start.49) | collective-permute-done | bytes 72 | tf_op jit(solution)/shard_map/ppermute | solution.py:28
  281.2 5.6 %collective-permute-start.51 = (f32[1,256]{1,0:T(1,128)S(1)}, f32[1,256]{1,0:T(1,128)S(1)}, u32[]{:S(2)}, u32[]{:S(2)}) collective-permute-start(f32[1,256]{1,0:T(1,128)S(1)} %get-tuple-element.172), channel_id=1, source_target_pairs={{16,0},{32,16},{48,32},{64,48},{80,64},{96,80},{112,96},{0,112},{1... | collective-permute-start | bytes 3080 | tf_op jit(solution)/shard_map/ppermute | solution.py:30
  286.8 3.3 %pad_maximum_fusion.6 = f32[62,10,258]{2,1,0:T(8,128)} fusion(f32[62,12,2]{2,1,0:T(8,128)} %collective-permute-done.22, f32[62,2,256]{2,1,0:T(2,128)S(1)} %copy-done.31, f32[62,8,256]{2,1,0:T(8,128)S(1)} %copy-done.21, f32[62,2,256]{2,1,0:T(2,128)S(1)} %copy-done.29), kind=kLoop, calls=%fused_computation.12 | loop fusion | flops 479880 | bytes 1407648 | tf_op jit(solution)/shard_map/concatenate | solution.py:26
  291.6 3.9 %collective-permute-done.53 = f32[10,1]{1,0:T(8,128)S(1)} collective-permute-done((f32[10,1]{1,0:T(8,128)S(1)}, f32[10,1]{1,0:T(8,128)S(1)}, u32[]{:S(2)}, u32[]{:S(2)}) %collective-permute-start.53) | collective-permute-done | bytes 72 | tf_op jit(solution)/shard_map/ppermute | solution.py:28
  297.5 5.6 %collective-permute-start.55 = (f32[1,256]{1,0:T(1,128)}, f32[1,256]{1,0:T(1,128)}, u32[]{:S(2)}, u32[]{:S(2)}) collective-permute-start(f32[1,256]{1,0:T(1,128)} %get-tuple-element.170), channel_id=1, source_target_pairs={{16,0},{32,16},{48,32},{64,48},{80,64},{96,80},{112,96},{0,112},{1... | collective-permute-start | bytes 3080 | tf_op jit(solution)/shard_map/ppermute | solution.py:30
  303.1 9.4 %fusion.79 = f32[62,8,256]{2,1,0:T(8,128)} fusion(f32[62,8,256]{2,1,0:T(8,128)} %param.9, f32[62,8,256]{2,1,0:T(8,128)} %get-tuple-element.31, f32[62,10,258]{2,1,0:T(8,128)} %get-tuple-element.59, f32[62,8,256]{2,1,0:T(8,128)S(1)} %copy-done.15, f32[62,10,258]{2,1,0:T(8,128)} %get-tuple-element.60, f32[62,10,258]{2,1,0:T(8,128)} %get-tuple-element.58, ...), kind=kLoop, calls=%fused_computation.169 | loop fusion | flops 4190208 | bytes 11173888 | tf_op jit(solution)/shard_map/add | solution.py:205
  314.7 3.9 %collective-permute-done.57 = f32[10,1]{1,0:T(8,128)S(1)} collective-permute-done((f32[10,1]{1,0:T(8,128)S(1)}, f32[10,1]{1,0:T(8,128)S(1)}, u32[]{:S(2)}, u32[]{:S(2)}) %collective-permute-start.57) | collective-permute-done | bytes 72 | tf_op jit(solution)/shard_map/ppermute | solution.py:28
  (310 shorter events, 76.2 us)
Async XLA Ops:
  2.1 33.9 %collective-permute-start.4 = (f32[62,2,256]{2,1,0:T(2,128)S(1)}, f32[62,2,256]{2,1,0:T(2,128)S(1)}, u32[]{:S(2)}, u32[]{:S(2)}) collective-permute-start(f32[62,2,256]{2,1,0:T(2,128)S(1)} %get-tuple-element.141), channel_id=1, source_target_pairs={{0,16},{16,32},{32,48},{48,64},{64,80},{80,96},{96,112},{112,0},{1... | collective-permute-start | bytes 380936 | tf_op jit(solution)/shard_map/ppermute | solution.py:28
  4.1 37.6 %collective-permute-start.5 = (f32[62,2,256]{2,1,0:T(2,128)S(1)}, f32[62,2,256]{2,1,0:T(2,128)S(1)}, u32[]{:S(2)}, u32[]{:S(2)}) collective-permute-start(f32[62,2,256]{2,1,0:T(2,128)S(1)} %get-tuple-element.142), channel_id=1, source_target_pairs={{16,0},{32,16},{48,32},{64,48},{80,64},{96,80},{112,96},{0,112},{1... | collective-permute-start | bytes 380936 | tf_op jit(solution)/shard_map/ppermute | solution.py:30
  8.6 11.5 %collective-permute-start = (s32[5,256]{1,0:T(8,128)S(1)}, s32[5,256]{1,0:T(8,128)S(1)}, u32[]{:S(2)}, u32[]{:S(2)}) collective-permute-start(s32[5,256]{1,0:T(8,128)S(1)} %get-tuple-element.181), channel_id=1, source_target_pairs={{0,16},{16,32},{32,48},{48,64},{64,80},{80,96},{96,112},{112,0},{1... | collective-permute-start | bytes 15368 | tf_op jit(solution)/shard_map/ppermute | solution.py:28
  9.4 8.6 %collective-permute-start.42 = (f32[1,256]{1,0:T(1,128)S(1)}, f32[1,256]{1,0:T(1,128)S(1)}, u32[]{:S(2)}, u32[]{:S(2)}) collective-permute-start(f32[1,256]{1,0:T(1,128)S(1)} %get-tuple-element.179), channel_id=1, source_target_pairs={{0,16},{16,32},{32,48},{48,64},{64,80},{80,96},{96,112},{112,0},{1... | collective-permute-start | bytes 3080 | tf_op jit(solution)/shard_map/ppermute | solution.py:28
  9.6 10.4 %collective-permute-start.43 = (f32[1,256]{1,0:T(1,128)S(1)}, f32[1,256]{1,0:T(1,128)S(1)}, u32[]{:S(2)}, u32[]{:S(2)}) collective-permute-start(f32[1,256]{1,0:T(1,128)S(1)} %get-tuple-element.180), channel_id=1, source_target_pairs={{16,0},{32,16},{48,32},{64,48},{80,64},{96,80},{112,96},{0,112},{1... | collective-permute-start | bytes 3080 | tf_op jit(solution)/shard_map/ppermute | solution.py:30
  20.0 22.1 %collective-permute-start.12 = (f32[62,2,256]{2,1,0:T(2,128)S(1)}, f32[62,2,256]{2,1,0:T(2,128)S(1)}, u32[]{:S(2)}, u32[]{:S(2)}) collective-permute-start(f32[62,2,256]{2,1,0:T(2,128)S(1)} %get-tuple-element.133), channel_id=1, source_target_pairs={{0,16},{16,32},{32,48},{48,64},{64,80},{80,96},{96,112},{112,0},{1... | collective-permute-start | bytes 380936 | tf_op jit(solution)/shard_map/ppermute | solution.py:28
  26.8 6.9 %collective-permute-start.3 = (s32[18,5]{1,0:T(8,128)S(1)}, s32[18,5]{1,0:T(8,128)S(1)}, u32[]{:S(2)}, u32[]{:S(2)}) collective-permute-start(s32[18,5]{1,0:T(8,128)S(1)} %get-tuple-element.150), channel_id=1, source_target_pairs={{1,0},{2,1},{3,2},{4,3},{5,4},{6,5},{7,6},{8,7},{9,8},{10,9},{11,1... | collective-permute-start | bytes 1088 | tf_op jit(solution)/shard_map/ppermute | solution.py:30
  27.8 20.1 %collective-permute-start.13 = (f32[62,2,256]{2,1,0:T(2,128)S(1)}, f32[62,2,256]{2,1,0:T(2,128)S(1)}, u32[]{:S(2)}, u32[]{:S(2)}) collective-permute-start(f32[62,2,256]{2,1,0:T(2,128)S(1)} %get-tuple-element.134), channel_id=1, source_target_pairs={{16,0},{32,16},{48,32},{64,48},{80,64},{96,80},{112,96},{0,112},{1... | collective-permute-start | bytes 380936 | tf_op jit(solution)/shard_map/ppermute | solution.py:30
  33.7 14.5 %collective-permute-start.8 = (f32[62,2,256]{2,1,0:T(2,128)S(1)}, f32[62,2,256]{2,1,0:T(2,128)S(1)}, u32[]{:S(2)}, u32[]{:S(2)}) collective-permute-start(f32[62,2,256]{2,1,0:T(2,128)S(1)} %get-tuple-element.139), channel_id=1, source_target_pairs={{0,16},{16,32},{32,48},{48,64},{64,80},{80,96},{96,112},{112,0},{1... | collective-permute-start | bytes 380936 | tf_op jit(solution)/shard_map/ppermute | solution.py:28
  36.0 16.2 %collective-permute-start.9 = (f32[62,2,256]{2,1,0:T(2,128)S(1)}, f32[62,2,256]{2,1,0:T(2,128)S(1)}, u32[]{:S(2)}, u32[]{:S(2)}) collective-permute-start(f32[62,2,256]{2,1,0:T(2,128)S(1)} %get-tuple-element.140), channel_id=1, source_target_pairs={{16,0},{32,16},{48,32},{64,48},{80,64},{96,80},{112,96},{0,112},{1... | collective-permute-start | bytes 380936 | tf_op jit(solution)/shard_map/ppermute | solution.py:30
  41.7 10.9 %collective-permute-start.16 = (f32[62,2,256]{2,1,0:T(2,128)S(1)}, f32[62,2,256]{2,1,0:T(2,128)S(1)}, u32[]{:S(2)}, u32[]{:S(2)}) collective-permute-start(f32[62,2,256]{2,1,0:T(2,128)S(1)} %get-tuple-element.135), channel_id=1, source_target_pairs={{0,16},{16,32},{32,48},{48,64},{64,80},{80,96},{96,112},{112,0},{1... | collective-permute-start | bytes 380936 | tf_op jit(solution)/shard_map/ppermute | solution.py:28
  42.2 14.4 %collective-permute-start.17 = (f32[62,2,256]{2,1,0:T(2,128)S(1)}, f32[62,2,256]{2,1,0:T(2,128)S(1)}, u32[]{:S(2)}, u32[]{:S(2)}) collective-permute-start(f32[62,2,256]{2,1,0:T(2,128)S(1)} %get-tuple-element.136), channel_id=1, source_target_pairs={{16,0},{32,16},{48,32},{64,48},{80,64},{96,80},{112,96},{0,112},{1... | collective-permute-start | bytes 380936 | tf_op jit(solution)/shard_map/ppermute | solution.py:30
  47.9 10.5 %collective-permute-start.6 = (f32[62,12,2]{2,1,0:T(8,128)S(1)}, f32[62,12,2]{2,1,0:T(8,128)S(1)}, u32[]{:S(2)}, u32[]{:S(2)}) collective-permute-start(f32[62,12,2]{2,1,0:T(8,128)S(1)} %get-tuple-element.125), channel_id=1, source_target_pairs={{0,1},{1,2},{2,3},{3,4},{4,5},{5,6},{6,7},{7,8},{8,9},{9,10},{10,1... | collective-permute-start | bytes 17864 | tf_op jit(solution)/shard_map/ppermute | solution.py:28
  48.3 13.5 %collective-permute-start.7 = (f32[62,12,2]{2,1,0:T(8,128)S(1)}, f32[62,12,2]{2,1,0:T(8,128)S(1)}, u32[]{:S(2)}, u32[]{:S(2)}) collective-permute-start(f32[62,12,2]{2,1,0:T(8,128)S(1)} %get-tuple-element.126), channel_id=1, source_target_pairs={{1,0},{2,1},{3,2},{4,3},{5,4},{6,5},{7,6},{8,7},{9,8},{10,9},{11,1... | collective-permute-start | bytes 17864 | tf_op jit(solution)/shard_map/ppermute | solution.py:30
  52.2 27.3 %collective-permute-start.15 = (f32[62,12,2]{2,1,0:T(8,128)S(1)}, f32[62,12,2]{2,1,0:T(8,128)S(1)}, u32[]{:S(2)}, u32[]{:S(2)}) collective-permute-start(f32[62,12,2]{2,1,0:T(8,128)S(1)} %get-tuple-element.117), channel_id=1, source_target_pairs={{0,1},{1,2},{2,3},{3,4},{4,5},{5,6},{6,7},{7,8},{8,9},{9,10},{10,1... | collective-permute-start | bytes 17864 | tf_op jit(solution)/shard_map/ppermute | solution.py:28
  52.6 29.1 %collective-permute-start.14 = (f32[62,12,2]{2,1,0:T(8,128)S(1)}, f32[62,12,2]{2,1,0:T(8,128)S(1)}, u32[]{:S(2)}, u32[]{:S(2)}) collective-permute-start(f32[62,12,2]{2,1,0:T(8,128)S(1)} %get-tuple-element.118), channel_id=1, source_target_pairs={{1,0},{2,1},{3,2},{4,3},{5,4},{6,5},{7,6},{8,7},{9,8},{10,9},{11,1... | collective-permute-start | bytes 17864 | tf_op jit(solution)/shard_map/ppermute | solution.py:30
  56.5 12.7 %collective-permute-start.10 = (f32[62,12,2]{2,1,0:T(8,128)S(1)}, f32[62,12,2]{2,1,0:T(8,128)S(1)}, u32[]{:S(2)}, u32[]{:S(2)}) collective-permute-start(f32[62,12,2]{2,1,0:T(8,128)S(1)} %get-tuple-element.123), channel_id=1, source_target_pairs={{0,1},{1,2},{2,3},{3,4},{4,5},{5,6},{6,7},{7,8},{8,9},{9,10},{10,1... | collective-permute-start | bytes 17864 | tf_op jit(solution)/shard_map/ppermute | solution.py:28
  58.4 11.2 %collective-permute-start.11 = (f32[62,12,2]{2,1,0:T(8,128)S(1)}, f32[62,12,2]{2,1,0:T(8,128)S(1)}, u32[]{:S(2)}, u32[]{:S(2)}) collective-permute-start(f32[62,12,2]{2,1,0:T(8,128)S(1)} %get-tuple-element.124), channel_id=1, source_target_pairs={{1,0},{2,1},{3,2},{4,3},{5,4},{6,5},{7,6},{8,7},{9,8},{10,9},{11,1... | collective-permute-start | bytes 17864 | tf_op jit(solution)/shard_map/ppermute | solution.py:30
  61.8 30.9 %collective-permute-start.19 = (f32[62,12,2]{2,1,0:T(8,128)}, f32[62,12,2]{2,1,0:T(8,128)S(1)}, u32[]{:S(2)}, u32[]{:S(2)}) collective-permute-start(f32[62,12,2]{2,1,0:T(8,128)} %get-tuple-element.119), channel_id=1, source_target_pairs={{0,1},{1,2},{2,3},{3,4},{4,5},{5,6},{6,7},{7,8},{8,9},{9,10},{10,1... | collective-permute-start | bytes 17864 | tf_op jit(solution)/shard_map/ppermute | solution.py:28
  69.3 26.5 %collective-permute-start.18 = (f32[62,12,2]{2,1,0:T(8,128)}, f32[62,12,2]{2,1,0:T(8,128)}, u32[]{:S(2)}, u32[]{:S(2)}) collective-permute-start(f32[62,12,2]{2,1,0:T(8,128)} %get-tuple-element.120), channel_id=1, source_target_pairs={{1,0},{2,1},{3,2},{4,3},{5,4},{6,5},{7,6},{8,7},{9,8},{10,9},{11,1... | collective-permute-start | bytes 17864 | tf_op jit(solution)/shard_map/ppermute | solution.py:30
  134.5 26.9 %collective-permute-start.24 = (f32[62,2,256]{2,1,0:T(2,128)}, f32[62,2,256]{2,1,0:T(2,128)}, u32[]{:S(2)}, u32[]{:S(2)}) collective-permute-start(f32[62,2,256]{2,1,0:T(2,128)} %get-tuple-element.137), channel_id=1, source_target_pairs={{0,16},{16,32},{32,48},{48,64},{64,80},{80,96},{96,112},{112,0},{1... | collective-permute-start | bytes 380936 | tf_op jit(solution)/shard_map/ppermute | solution.py:28
  134.5 26.9 %collective-permute-start.25 = (f32[62,2,256]{2,1,0:T(2,128)}, f32[62,2,256]{2,1,0:T(2,128)}, u32[]{:S(2)}, u32[]{:S(2)}) collective-permute-start(f32[62,2,256]{2,1,0:T(2,128)} %get-tuple-element.138), channel_id=1, source_target_pairs={{16,0},{32,16},{48,32},{64,48},{80,64},{96,80},{112,96},{0,112},{1... | collective-permute-start | bytes 380936 | tf_op jit(solution)/shard_map/ppermute | solution.py:30
  154.0 12.8 %collective-permute-start.20 = (f32[62,2,256]{2,1,0:T(2,128)S(1)}, f32[62,2,256]{2,1,0:T(2,128)S(1)}, u32[]{:S(2)}, u32[]{:S(2)}) collective-permute-start(f32[62,2,256]{2,1,0:T(2,128)S(1)} %get-tuple-element.129), channel_id=1, source_target_pairs={{0,16},{16,32},{32,48},{48,64},{64,80},{80,96},{96,112},{112,0},{1... | collective-permute-start | bytes 380936 | tf_op jit(solution)/shard_map/ppermute | solution.py:28
  154.3 12.6 %collective-permute-start.21 = (f32[62,2,256]{2,1,0:T(2,128)S(1)}, f32[62,2,256]{2,1,0:T(2,128)S(1)}, u32[]{:S(2)}, u32[]{:S(2)}) collective-permute-start(f32[62,2,256]{2,1,0:T(2,128)S(1)} %get-tuple-element.130), channel_id=1, source_target_pairs={{16,0},{32,16},{48,32},{64,48},{80,64},{96,80},{112,96},{0,112},{1... | collective-permute-start | bytes 380936 | tf_op jit(solution)/shard_map/ppermute | solution.py:30
  163.0 10.6 %collective-permute-start.26 = (f32[62,12,2]{2,1,0:T(8,128)S(1)}, f32[62,12,2]{2,1,0:T(8,128)S(1)}, u32[]{:S(2)}, u32[]{:S(2)}) collective-permute-start(f32[62,12,2]{2,1,0:T(8,128)S(1)} %get-tuple-element.121), channel_id=1, source_target_pairs={{0,1},{1,2},{2,3},{3,4},{4,5},{5,6},{6,7},{7,8},{8,9},{9,10},{10,1... | collective-permute-start | bytes 17864 | tf_op jit(solution)/shard_map/ppermute | solution.py:28
  163.1 13.8 %collective-permute-start.27 = (f32[62,12,2]{2,1,0:T(8,128)S(1)}, f32[62,12,2]{2,1,0:T(8,128)S(1)}, u32[]{:S(2)}, u32[]{:S(2)}) collective-permute-start(f32[62,12,2]{2,1,0:T(8,128)S(1)} %get-tuple-element.122), channel_id=1, source_target_pairs={{1,0},{2,1},{3,2},{4,3},{5,4},{6,5},{7,6},{8,7},{9,8},{10,9},{11,1... | collective-permute-start | bytes 17864 | tf_op jit(solution)/shard_map/ppermute | solution.py:30
  168.2 33.4 %collective-permute-start.22 = (f32[62,12,2]{2,1,0:T(8,128)}, f32[62,12,2]{2,1,0:T(8,128)}, u32[]{:S(2)}, u32[]{:S(2)}) collective-permute-start(f32[62,12,2]{2,1,0:T(8,128)} %get-tuple-element.113), channel_id=1, source_target_pairs={{0,1},{1,2},{2,3},{3,4},{4,5},{5,6},{6,7},{7,8},{8,9},{9,10},{10,1... | collective-permute-start | bytes 17864 | tf_op jit(solution)/shard_map/ppermute | solution.py:28
  168.2 33.4 %collective-permute-start.23 = (f32[62,12,2]{2,1,0:T(8,128)}, f32[62,12,2]{2,1,0:T(8,128)}, u32[]{:S(2)}, u32[]{:S(2)}) collective-permute-start(f32[62,12,2]{2,1,0:T(8,128)} %get-tuple-element.114), channel_id=1, source_target_pairs={{1,0},{2,1},{3,2},{4,3},{5,4},{6,5},{7,6},{8,7},{9,8},{10,9},{11,1... | collective-permute-start | bytes 17864 | tf_op jit(solution)/shard_map/ppermute | solution.py:30
  195.5 16.7 %collective-permute-start.28 = (f32[62,2,256]{2,1,0:T(2,128)S(1)}, f32[62,2,256]{2,1,0:T(2,128)S(1)}, u32[]{:S(2)}, u32[]{:S(2)}) collective-permute-start(f32[62,2,256]{2,1,0:T(2,128)S(1)} %get-tuple-element.127), channel_id=1, source_target_pairs={{0,16},{16,32},{32,48},{48,64},{64,80},{80,96},{96,112},{112,0},{1... | collective-permute-start | bytes 380936 | tf_op jit(solution)/shard_map/ppermute | solution.py:28
  195.7 16.6 %collective-permute-start.29 = (f32[62,2,256]{2,1,0:T(2,128)S(1)}, f32[62,2,256]{2,1,0:T(2,128)S(1)}, u32[]{:S(2)}, u32[]{:S(2)}) collective-permute-start(f32[62,2,256]{2,1,0:T(2,128)S(1)} %get-tuple-element.128), channel_id=1, source_target_pairs={{16,0},{32,16},{48,32},{64,48},{80,64},{96,80},{112,96},{0,112},{1... | collective-permute-start | bytes 380936 | tf_op jit(solution)/shard_map/ppermute | solution.py:30
  206.5 10.0 %collective-permute-start.32 = (f32[62,2,256]{2,1,0:T(2,128)S(1)}, f32[62,2,256]{2,1,0:T(2,128)S(1)}, u32[]{:S(2)}, u32[]{:S(2)}) collective-permute-start(f32[62,2,256]{2,1,0:T(2,128)S(1)} %get-tuple-element.131), channel_id=1, source_target_pairs={{0,16},{16,32},{32,48},{48,64},{64,80},{80,96},{96,112},{112,0},{1... | collective-permute-start | bytes 380936 | tf_op jit(solution)/shard_map/ppermute | solution.py:28
  206.6 10.0 %collective-permute-start.33 = (f32[62,2,256]{2,1,0:T(2,128)S(1)}, f32[62,2,256]{2,1,0:T(2,128)S(1)}, u32[]{:S(2)}, u32[]{:S(2)}) collective-permute-start(f32[62,2,256]{2,1,0:T(2,128)S(1)} %get-tuple-element.132), channel_id=1, source_target_pairs={{16,0},{32,16},{48,32},{64,48},{80,64},{96,80},{112,96},{0,112},{1... | collective-permute-start | bytes 380936 | tf_op jit(solution)/shard_map/ppermute | solution.py:30
  212.6 10.6 %collective-permute-start.31 = (f32[62,12,2]{2,1,0:T(8,128)S(1)}, f32[62,12,2]{2,1,0:T(8,128)S(1)}, u32[]{:S(2)}, u32[]{:S(2)}) collective-permute-start(f32[62,12,2]{2,1,0:T(8,128)S(1)} %get-tuple-element.111), channel_id=1, source_target_pairs={{0,1},{1,2},{2,3},{3,4},{4,5},{5,6},{6,7},{7,8},{8,9},{9,10},{10,1... | collective-permute-start | bytes 17864 | tf_op jit(solution)/shard_map/ppermute | solution.py:28
  212.7 12.8 %collective-permute-start.30 = (f32[62,12,2]{2,1,0:T(8,128)S(1)}, f32[62,12,2]{2,1,0:T(8,128)S(1)}, u32[]{:S(2)}, u32[]{:S(2)}) collective-permute-start(f32[62,12,2]{2,1,0:T(8,128)S(1)} %get-tuple-element.112), channel_id=1, source_target_pairs={{1,0},{2,1},{3,2},{4,3},{5,4},{6,5},{7,6},{8,7},{9,8},{10,9},{11,1... | collective-permute-start | bytes 17864 | tf_op jit(solution)/shard_map/ppermute | solution.py:30
  217.8 18.3 %collective-permute-start.35 = (f32[62,12,2]{2,1,0:T(8,128)}, f32[62,12,2]{2,1,0:T(8,128)S(1)}, u32[]{:S(2)}, u32[]{:S(2)}) collective-permute-start(f32[62,12,2]{2,1,0:T(8,128)} %get-tuple-element.115), channel_id=1, source_target_pairs={{0,1},{1,2},{2,3},{3,4},{4,5},{5,6},{6,7},{7,8},{8,9},{9,10},{10,1... | collective-permute-start | bytes 17864 | tf_op jit(solution)/shard_map/ppermute | solution.py:28
  217.8 21.3 %collective-permute-start.34 = (f32[62,12,2]{2,1,0:T(8,128)}, f32[62,12,2]{2,1,0:T(8,128)S(1)}, u32[]{:S(2)}, u32[]{:S(2)}) collective-permute-start(f32[62,12,2]{2,1,0:T(8,128)} %get-tuple-element.116), channel_id=1, source_target_pairs={{1,0},{2,1},{3,2},{4,3},{5,4},{6,5},{7,6},{8,7},{9,8},{10,9},{11,1... | collective-permute-start | bytes 17864 | tf_op jit(solution)/shard_map/ppermute | solution.py:30
  250.8 7.7 %collective-permute-start.36 = (f32[1,256]{1,0:T(1,128)S(1)}, f32[1,256]{1,0:T(1,128)S(1)}, u32[]{:S(2)}, u32[]{:S(2)}) collective-permute-start(f32[1,256]{1,0:T(1,128)S(1)} %get-tuple-element.175), channel_id=1, source_target_pairs={{0,16},{16,32},{32,48},{48,64},{64,80},{80,96},{96,112},{112,0},{1... | collective-permute-start | bytes 3080 | tf_op jit(solution)/shard_map/ppermute | solution.py:28
  250.9 7.7 %collective-permute-start.37 = (f32[1,256]{1,0:T(1,128)S(1)}, f32[1,256]{1,0:T(1,128)S(1)}, u32[]{:S(2)}, u32[]{:S(2)}) collective-permute-start(f32[1,256]{1,0:T(1,128)S(1)} %get-tuple-element.176), channel_id=1, source_target_pairs={{16,0},{32,16},{48,32},{64,48},{80,64},{96,80},{112,96},{0,112},{1... | collective-permute-start | bytes 3080 | tf_op jit(solution)/shard_map/ppermute | solution.py:30
  256.6 7.2 %collective-permute-start.41 = (f32[1,256]{1,0:T(1,128)S(1)}, f32[1,256]{1,0:T(1,128)S(1)}, u32[]{:S(2)}, u32[]{:S(2)}) collective-permute-start(f32[1,256]{1,0:T(1,128)S(1)} %get-tuple-element.178), channel_id=1, source_target_pairs={{0,16},{16,32},{32,48},{48,64},{64,80},{80,96},{96,112},{112,0},{1... | collective-permute-start | bytes 3080 | tf_op jit(solution)/shard_map/ppermute | solution.py:28
  264.3 11.2 %collective-permute-start.46 = (f32[1,256]{1,0:T(1,128)S(1)}, f32[1,256]{1,0:T(1,128)S(1)}, u32[]{:S(2)}, u32[]{:S(2)}) collective-permute-start(f32[1,256]{1,0:T(1,128)S(1)} %get-tuple-element.173), channel_id=1, source_target_pairs={{0,16},{16,32},{32,48},{48,64},{64,80},{80,96},{96,112},{112,0},{1... | collective-permute-start | bytes 3080 | tf_op jit(solution)/shard_map/ppermute | solution.py:28
  264.4 11.1 %collective-permute-start.47 = (f32[1,256]{1,0:T(1,128)S(1)}, f32[1,256]{1,0:T(1,128)S(1)}, u32[]{:S(2)}, u32[]{:S(2)}) collective-permute-start(f32[1,256]{1,0:T(1,128)S(1)} %get-tuple-element.174), channel_id=1, source_target_pairs={{16,0},{32,16},{48,32},{64,48},{80,64},{96,80},{112,96},{0,112},{1... | collective-permute-start | bytes 3080 | tf_op jit(solution)/shard_map/ppermute | solution.py:30
  275.6 5.3 %collective-permute-start.49 = (f32[10,1]{1,0:T(8,128)S(1)}, f32[10,1]{1,0:T(8,128)S(1)}, u32[]{:S(2)}, u32[]{:S(2)}) collective-permute-start(f32[10,1]{1,0:T(8,128)S(1)} %get-tuple-element.156), channel_id=1, source_target_pairs={{0,1},{1,2},{2,3},{3,4},{4,5},{5,6},{6,7},{7,8},{8,9},{9,10},{10,1... | collective-permute-start | bytes 128 | tf_op jit(solution)/shard_map/ppermute | solution.py:28
  281.1 9.0 %collective-permute-start.50 = (f32[1,256]{1,0:T(1,128)S(1)}, f32[1,256]{1,0:T(1,128)S(1)}, u32[]{:S(2)}, u32[]{:S(2)}) collective-permute-start(f32[1,256]{1,0:T(1,128)S(1)} %get-tuple-element.171), channel_id=1, source_target_pairs={{0,16},{16,32},{32,48},{48,64},{64,80},{80,96},{96,112},{112,0},{1... | collective-permute-start | bytes 3080 | tf_op jit(solution)/shard_map/ppermute | solution.py:28
  281.2 8.9 %collective-permute-start.51 = (f32[1,256]{1,0:T(1,128)S(1)}, f32[1,256]{1,0:T(1,128)S(1)}, u32[]{:S(2)}, u32[]{:S(2)}) collective-permute-start(f32[1,256]{1,0:T(1,128)S(1)} %get-tuple-element.172), channel_id=1, source_target_pairs={{16,0},{32,16},{48,32},{64,48},{80,64},{96,80},{112,96},{0,112},{1... | collective-permute-start | bytes 3080 | tf_op jit(solution)/shard_map/ppermute | solution.py:30
  290.2 5.3 %collective-permute-start.53 = (f32[10,1]{1,0:T(8,128)S(1)}, f32[10,1]{1,0:T(8,128)S(1)}, u32[]{:S(2)}, u32[]{:S(2)}) collective-permute-start(f32[10,1]{1,0:T(8,128)S(1)} %get-tuple-element.154), channel_id=1, source_target_pairs={{0,1},{1,2},{2,3},{3,4},{4,5},{5,6},{6,7},{7,8},{8,9},{9,10},{10,1... | collective-permute-start | bytes 128 | tf_op jit(solution)/shard_map/ppermute | solution.py:28
  297.5 15.0 %collective-permute-start.54 = (f32[1,256]{1,0:T(1,128)}, f32[1,256]{1,0:T(1,128)}, u32[]{:S(2)}, u32[]{:S(2)}) collective-permute-start(f32[1,256]{1,0:T(1,128)} %get-tuple-element.169), channel_id=1, source_target_pairs={{0,16},{16,32},{32,48},{48,64},{64,80},{80,96},{96,112},{112,0},{1... | collective-permute-start | bytes 3080 | tf_op jit(solution)/shard_map/ppermute | solution.py:28
  297.5 15.0 %collective-permute-start.55 = (f32[1,256]{1,0:T(1,128)}, f32[1,256]{1,0:T(1,128)}, u32[]{:S(2)}, u32[]{:S(2)}) collective-permute-start(f32[1,256]{1,0:T(1,128)} %get-tuple-element.170), channel_id=1, source_target_pairs={{16,0},{32,16},{48,32},{64,48},{80,64},{96,80},{112,96},{0,112},{1... | collective-permute-start | bytes 3080 | tf_op jit(solution)/shard_map/ppermute | solution.py:30
  313.3 5.3 %collective-permute-start.57 = (f32[10,1]{1,0:T(8,128)S(1)}, f32[10,1]{1,0:T(8,128)S(1)}, u32[]{:S(2)}, u32[]{:S(2)}) collective-permute-start(f32[10,1]{1,0:T(8,128)S(1)} %get-tuple-element.152), channel_id=1, source_target_pairs={{0,1},{1,2},{2,3},{3,4},{4,5},{5,6},{6,7},{7,8},{8,9},{9,10},{10,1... | collective-permute-start | bytes 128 | tf_op jit(solution)/shard_map/ppermute | solution.py:28
  (77 other events, 985.8 us)
where the time goes:
time: 328 us; the launch traced here: 322 us
  other arithmetic  151 us (46%)
  starting transfers between devices  110 us (34%)
  waiting for transfers between devices  34.5 us (11%)
  local copies, waits for them, and re-layouts  24 us (7%)
    ppermute x29, starting transfers between devices, extended(): lax.ppermute(head, axis, [((i + 1) % count, i) for i in range(count)])  102 us
    slice x8, other arithmetic, sides(): field[..., 1:-1, 1:-1]  46.8 us
    concatenate x34, other arithmetic, extended(): jnp.concatenate([lax.ppermute(tail, axis, [(i, (i + 1) % count) for i in...  38 us
    ppermute x29, waiting for transfers between devices, extended(): lax.ppermute(tail, axis, [(i, (i + 1) % count) for i in range(count)])  29.5 us
    add x2, other arithmetic, body(): item + 0.5 * (term_first + term_second)  18.9 us
    add x2, other arithmetic, body(): item + extra  18.5 us
    slice x23, local copies, waits for them, and re-layouts, extended(): lax.slice_in_dim(cells, cells.shape[dim] - width, cells.shape[dim], axis=...  15.4 us
    mul x2, other arithmetic, tendency(): east_tend = inner * (rotate * north_in - press_x + mixing(east_vel))  9.77 us
  transfers between devices with their start and end apart: 58, of which 18 were waited for; matrix products, arithmetic and copies ran while one was open for 36% of the time, Pallas kernels for 0%

commit v1 on v0

v1 whole, which is shorter than its diff:
```python
import functools
import math

import jax
import jax.numpy as jnp
from jax import lax
from jax.experimental import pallas as pl
from jax.experimental.pallas import tpu as pltpu
from jax.sharding import PartitionSpec as P

ITERS = 4
KAPPA = 0.004
ADVECT = 0.25
PRESS = 0.1
WIND = 0.5
PHI = 0.5
DIVERGE = 2.0
LOWER = 0.2
UPPER = 2.0

MESH = pl.DeviceIdType.MESH
FIELDS = 4
HALO = 4
SUB = 8
LANE = 128
AHEAD = 2
UNROLL = 2


def chebyshev_weights(count):
    middle = 0.5 * (UPPER + LOWER)
    half_span = 0.5 * (UPPER - LOWER)
    ratio_value = middle / half_span
    rho_now = 1.0 / ratio_value
    updates = []
    for _ in range(count - 1):
        rho_next = 1.0 / (2.0 * ratio_value - rho_now)
        updates.append((rho_next * rho_now, 2.0 * rho_next / half_span))
        rho_now = rho_next
    return 1.0 / middle, updates


def east(x):
    return pltpu.roll(x, x.shape[1] - 1, 1)


def west(x):
    return pltpu.roll(x, 1, 1)


def north(x):
    return pltpu.roll(x, x.shape[0] - 1, 0)


def south(x):
    return pltpu.roll(x, 1, 0)


def slot_lane(field, row):
    return (field % 2) * 64 + row * 8 + (field // 2) * 4


def turn(x, shift):
    shift = shift % LANE
    return x if shift == 0 else pltpu.roll(x, shift, 1)


def rows_loop(first, last, unroll, body):
    count = last - first
    assert count % unroll == 0

    def step(index, carry):
        for k in range(unroll):
            body(first + index * unroll + k)
        return carry

    lax.fori_loop(0, count // unroll, step, 0)


def kernel(
    levels, total_rows, by_count, bx_count,
    u_in, v_in, t_in, s_in, wind_in, ssh_in, depth_in,
    u_out, v_out, t_out, s_out, surface_out,
    own, ext, pack_send, pack_recv, corner_send, corner_recv, edge,
    lap, mix, press, mid, acc, carry_one, carry_two,
    depth_c, depth_e, depth_n, stress, cor,
    flow_sum, moved, moved_halo, flat,
    in_sem, out_sem, row_send, row_recv, pack_ss, pack_rs, corner_ss, corner_rs,
    moved_ss, moved_rs,
):
    inputs = (u_in, v_in, t_in, s_in)
    outputs = (u_out, v_out, t_out, s_out)
    rows = SUB
    span = rows + 2 * HALO
    width = ext.shape[-1]
    cols = width - LANE
    tiles = cols // LANE
    groups = -(-levels // SUB)
    flat_group = groups
    block = SUB * rows
    by = lax.axis_index("by")
    bx = lax.axis_index("bx")
    to_north = (lax.rem(by + 1, by_count), bx)
    to_south = (lax.rem(by + by_count - 1, by_count), bx)
    to_east = (by, lax.rem(bx + 1, bx_count))
    to_west = (by, lax.rem(bx + bx_count - 1, bx_count))

    def load_copy(field, tile):
        return pltpu.make_async_copy(
            inputs[field].at[:, pl.ds(tile * LANE, LANE)],
            own.at[field, tile, pl.ds(0, levels * rows)],
            in_sem.at[field, tile],
        )

    for field in range(FIELDS):
        for tile in range(tiles):
            load_copy(field, tile).start()

    barrier = pltpu.get_barrier_semaphore()
    for device in (to_north, to_south, to_east, to_west):
        pl.semaphore_signal(barrier, inc=1, device_id=device, device_id_type=MESH)

    base = groups * block
    for tile in range(tiles):
        lanes = slice(tile * LANE, (tile + 1) * LANE)
        own[0, tile, base : base + rows, :] = depth_in[:, lanes].astype(jnp.float32)
        own[0, tile, base + rows : base + 2 * rows, :] = ssh_in[:, lanes]
        own[0, tile, base + 2 * rows : base + 4 * rows, :] = wind_in[:, lanes]
        own[0, tile, base + 4 * rows : base + 8 * rows, :] = jnp.zeros((4 * rows, LANE), jnp.float32)
        if levels % SUB:
            pad = groups * block - levels * rows
            for field in range(FIELDS):
                own[field, tile, levels * rows : groups * block, :] = jnp.zeros((pad, LANE), jnp.float32)

    lane = lax.broadcasted_iota(jnp.int32, (SUB, LANE), 1)

    def stage(group, fields):
        west_pack = jnp.zeros((SUB, LANE), jnp.float32)
        east_pack = jnp.zeros((SUB, LANE), jnp.float32)
        for field in range(fields):
            for row in range(rows):
                parts = [
                    own[field, tile, pl.ds(group * block + row, SUB, stride=rows), :]
                    for tile in range(tiles)
                ]
                for tile in range(tiles):
                    ext[group, field, HALO + row, :, tile * LANE : (tile + 1) * LANE] = parts[tile]
                first = slot_lane(field, row)
                here = (lane >= first) & (lane < first + HALO)
                west_pack = jnp.where(here, turn(parts[0], first), west_pack)
                east_pack = jnp.where(here, turn(parts[-1], first + HALO), east_pack)
        pack_send[0, group] = west_pack
        pack_send[1, group] = east_pack

    def row_copy(group, fields, side):
        source = HALO + rows - HALO if side == 0 else HALO
        target = 0 if side == 0 else HALO + rows
        return pltpu.make_async_remote_copy(
            src_ref=ext.at[group, pl.ds(0, fields), pl.ds(source, HALO), :, pl.ds(0, cols)],
            dst_ref=ext.at[group, pl.ds(0, fields), pl.ds(target, HALO), :, pl.ds(0, cols)],
            send_sem=row_send.at[side, group],
            recv_sem=row_recv.at[side, group],
            device_id=to_north if side == 0 else to_south,
            device_id_type=MESH,
        )

    def pack_copy(side):
        return pltpu.make_async_remote_copy(
            src_ref=pack_send.at[side],
            dst_ref=pack_recv.at[1 - side],
            send_sem=pack_ss.at[side],
            recv_sem=pack_rs.at[1 - side],
            device_id=to_west if side == 0 else to_east,
            device_id_type=MESH,
        )

    def corner_copy(side):
        return pltpu.make_async_remote_copy(
            src_ref=corner_send.at[side],
            dst_ref=corner_recv.at[side],
            send_sem=corner_ss.at[side],
            recv_sem=corner_rs.at[side],
            device_id=to_north if side == 0 else to_south,
            device_id_type=MESH,
        )

    for field in range(FIELDS):
        for tile in range(tiles):
            load_copy(field, tile).wait()
    stage(flat_group, 1)
    pl.semaphore_wait(barrier, 4)
    for side in range(2):
        row_copy(flat_group, 1, side).start()
    for group in range(AHEAD):
        stage(group, FIELDS)
        for side in range(2):
            row_copy(group, FIELDS, side).start()

    def stage_step(group, carry):
        stage(group, FIELDS)
        return carry

    lax.fori_loop(AHEAD, groups, stage_step, 0)
    for side in range(2):
        pack_copy(side).start()

    row_index = by * rows - HALO + lax.broadcasted_iota(jnp.int32, (span, LANE), 0)
    turning = 1.2 * jnp.sin(0.9 * math.pi * ((row_index.astype(jnp.float32) + 0.5) / total_rows - 0.5))
    for row in range(span):
        one = jnp.broadcast_to(turning[row : row + 1, :], (SUB, LANE))
        for tile in range(width // LANE):
            cor[row, :, tile * LANE : (tile + 1) * LANE] = one

    for side in range(2):
        pack_copy(1 - side).wait_recv()
    own_lanes = (lane >= HALO * 8) & (lane < (HALO + rows) * 8)
    west_lanes = (lane & 7) < HALO

    def expand(group, fields):
        from_west = pack_recv[0, group]
        from_east = pack_recv[1, group]
        for_north = jnp.zeros((SUB, LANE), jnp.float32)
        for_south = jnp.zeros((SUB, LANE), jnp.float32)
        for field in range(fields):
            shift = HALO * 8 - slot_lane(field, 0)
            both = jnp.where(west_lanes, turn(from_west, shift), turn(from_east, shift + HALO))
            edge[group, field] = both
            part = (lane >= field * 32) & (lane < field * 32 + 32)
            for_north = jnp.where(part, turn(both, field * 32 - rows * 8), for_north)
            for_south = jnp.where(part, turn(both, field * 32 - HALO * 8), for_south)
        corner_send[0, group] = for_north
        corner_send[1, group] = for_south

    def expand_step(group, carry):
        expand(group, FIELDS)
        return carry

    expand(flat_group, 1)
    lax.fori_loop(0, groups, expand_step, 0)
    for side in range(2):
        corner_copy(side).start()

    def send_step(group, carry):
        for side in range(2):
            row_copy(group, FIELDS, side).start()
        return carry

    lax.fori_loop(AHEAD, groups, send_step, 0)

    for side in range(2):
        corner_copy(side).wait_recv()

    def widen(group, fields):
        from_south = corner_recv[0, group]
        from_north = corner_recv[1, group]
        for field in range(fields):
            all_rows = jnp.where(
                own_lanes,
                edge[group, field],
                jnp.where(lane < HALO * 8, turn(from_south, -32 * field), turn(from_north, 96 - 32 * field)),
            )
            for row in range(span):
                ext[group, field, row, :, cols:width] = turn(all_rows, LANE - HALO - 8 * row)

    for side in range(2):
        row_copy(flat_group, 1, side).wait_recv()
    widen(flat_group, 1)

    sub = lax.broadcasted_iota(jnp.int32, (SUB, width), 0)
    for row in range(span):
        index = by * rows + (row - HALO)
        inside = (index >= 0) & (index < total_rows)
        values = ext[flat_group, 0, row]
        here = jnp.where(inside, jnp.broadcast_to(values[0:1, :], (SUB, width)), 0.0)
        depth_c[row] = here
        depth_e[row] = jnp.minimum(here, east(here))
        for axis in range(2):
            stress[axis, row] = jnp.where(
                sub == 0, WIND * jnp.broadcast_to(values[2 + axis : 3 + axis, :], (SUB, width)), 0.0
            )
        carry_one[row] = jnp.zeros((SUB, width), jnp.float32)
        carry_two[row] = jnp.zeros((SUB, width), jnp.float32)
        place = (row + span - HALO) % span
        flat[0, place : place + 1, :] = here[0:1, :]
        flat[1, place : place + 1, :] = values[1:2, :]
    for row in range(span - 1):
        depth_n[row] = jnp.minimum(depth_c[row], depth_c[row + 1])
    for axis in range(2):
        for row in range(rows):
            flow_sum[axis, row] = jnp.zeros((SUB, cols), jnp.float32)

    depth = flat[0]
    ssh = flat[1]
    near = jnp.minimum(depth, east(depth))
    corner = jnp.minimum(near, north(near)) * (1.0 / levels)
    pair = corner + west(corner)
    diagonal_inverse = 1.0 / (PHI + 0.5 * (pair + south(pair)))
    ocean = jnp.where(depth > 0.0, 1.0, 0.0)

    def operator(field, corner):
        total = field + north(field)
        change = north(field) - field
        flux_x = corner * (0.5 * (east(total) - total))
        flux_y = corner * (0.5 * (east(change) + change))
        along_x = flux_x + south(flux_x)
        along_y = flux_y + west(flux_y)
        return PHI * field - 0.5 * ((along_x - west(along_x)) + (along_y - south(along_y)))

    flat[2] = corner
    flat[3] = diagonal_inverse
    flat[4] = ocean
    flat[5] = ocean * (PHI * ssh) - operator(ssh, corner)

    level = lax.broadcasted_iota(jnp.int32, (SUB, width), 0).astype(jnp.float32)

    def masks(group, row):
        number = level + (group * SUB).astype(jnp.float32)
        return (
            number < depth_c[row], number < depth_e[row],
            number < depth_n[row], number < depth_n[row - 1],
        )

    def first_half(state, row, group, carry):
        wet, wet_e, wet_n, wet_s = masks(group, row)
        east_vel = state(0, row)
        north_vel = state(1, row)
        for field in range(FIELDS):
            here = state(field, row)
            face_e = jnp.where(wet_e, east(here) - here, 0.0)
            face_w = west(face_e)
            face_n = jnp.where(wet_n, state(field, row + 1) - here, 0.0)
            face_s = jnp.where(wet_s, here - state(field, row - 1), 0.0)
            lap[field, row] = (face_e - face_w) + (face_n - face_s)
            mix[field, row] = (-0.5 * ADVECT) * (east_vel * (face_e + face_w) + north_vel * (face_n + face_s))
        density = jnp.where(wet, (-0.8 * PRESS) * state(2, row) + (0.6 * PRESS) * state(3, row), 0.0)
        running = density
        total = density
        for shift in (1, 2, 4):
            running = running + jnp.where(sub >= shift, pltpu.roll(running, shift, 0), 0.0)
            total = total + pltpu.roll(total, shift, 0)
        press[row] = carry[row] + running
        carry[row] = carry[row] + total

    def second_half(state, row, group, keep):
        wet, wet_e, wet_n, wet_s = masks(group, row)

        def faces(ref_row):
            here = ref_row(row)
            face_e = jnp.where(wet_e, east(here) - here, 0.0)
            face_n = jnp.where(wet_n, ref_row(row + 1) - here, 0.0)
            face_s = jnp.where(wet_s, here - ref_row(row - 1), 0.0)
            return face_e[:, :keep], west(face_e)[:, :keep], face_n[:, :keep], face_s[:, :keep]

        press_e, press_w, press_n, press_s = faces(lambda r: press[r])
        turned = cor[row][:, :keep]
        top = (group == 0).astype(jnp.float32)
        forced = (
            turned * state(1, row)[:, :keep] + top * stress[0, row][:, :keep],
            -turned * state(0, row)[:, :keep] + top * stress[1, row][:, :keep],
        )
        forced = [jnp.where(wet[:, :keep], item, 0.0) for item in forced]
        forced[0] = forced[0] - 0.5 * (press_e + press_w)
        forced[1] = forced[1] - 0.5 * (press_n + press_s)
        result = []
        for field in range(FIELDS):
            face_e, face_w, face_n, face_s = faces(lambda r: lap[field, r])
            change = mix[field, row][:, :keep] - KAPPA * ((face_e - face_w) + (face_n - face_s))
            result.append(change + forced[field] if field < 2 else change)
        return result

    def out_copy(group, field, tile, count):
        return pltpu.make_async_copy(
            own.at[field, tile, pl.ds(pl.multiple_of(group * block, block), count)],
            outputs[field].at[pl.ds(pl.multiple_of(group * block, block), count), pl.ds(tile * LANE, LANE)],
            out_sem.at[field, tile],
        )

    last_count = levels * rows - (groups - 1) * block

    def group_step(group, carry):
        for side in range(2):
            row_copy(group, FIELDS, side).wait_recv()
        widen(group, FIELDS)

        def given(field, row):
            return ext[group, field, row]

        def provisional(field, row):
            return mid[field, row]

        def pass_one(row):
            first_half(given, row, group, carry_one)

        def pass_two(row):
            first = second_half(given, row, group, width)
            for field in range(FIELDS):
                mid[field, row] = ext[group, field, row] + first[field]

        def pass_three(row):
            first_half(provisional, row, group, carry_two)

        def pass_four(row):
            second = second_half(provisional, row, group, cols)
            inner = row - HALO
            wet = (level + (group * SUB).astype(jnp.float32))[:, :cols] < depth_c[row][:, :cols]
            for field in range(FIELDS):
                value = 0.5 * (ext[group, field, row][:, :cols] + mid[field, row][:, :cols] + second[field])
                for tile in range(tiles):
                    own[field, tile, pl.ds(group * block + inner, SUB, stride=rows), :] = value[
                        :, tile * LANE : (tile + 1) * LANE
                    ]
                if field < 2:
                    flow_sum[field, inner] = flow_sum[field, inner] + jnp.where(wet, value, 0.0)

        rows_loop(1, span - 1, UNROLL, pass_one)
        rows_loop(2, span - 2, UNROLL, pass_two)
        rows_loop(3, span - 3, UNROLL, pass_three)
        rows_loop(HALO, HALO + rows, UNROLL, pass_four)

        @pl.when(group < groups - 1)
        def _():
            for field in range(FIELDS):
                for tile in range(tiles):
                    out_copy(group, field, tile, block).start()

        @pl.when(group == groups - 1)
        def _():
            for field in range(FIELDS):
                for tile in range(tiles):
                    out_copy(group, field, tile, last_count).start()

        return carry

    lax.fori_loop(0, groups, group_step, 0)

    for axis in range(2):
        for row in range(rows):
            moved[axis, row : row + 1, :cols] = jnp.sum(flow_sum[axis, row], axis=0, keepdims=True) * (1.0 / levels)

    def moved_column_copy(side):
        tile = 0 if side == 0 else tiles - 1
        return pltpu.make_async_remote_copy(
            src_ref=moved.at[:, :, pl.ds(tile * LANE, LANE)],
            dst_ref=moved_halo.at[1 - side, :, :, pl.ds(0, LANE)],
            send_sem=moved_ss.at[side],
            recv_sem=moved_rs.at[1 - side],
            device_id=to_west if side == 0 else to_east,
            device_id_type=MESH,
        )

    def moved_row_copy(side):
        return pltpu.make_async_remote_copy(
            src_ref=moved,
            dst_ref=moved_halo.at[2 + side],
            send_sem=moved_ss.at[2 + side],
            recv_sem=moved_rs.at[2 + side],
            device_id=to_north if side == 0 else to_south,
            device_id_type=MESH,
        )

    for side in range(2):
        moved_column_copy(side).start()
    for side in range(2):
        moved_column_copy(1 - side).wait_recv()
    for axis in range(2):
        moved[axis, :, cols:width] = jnp.where(
            lane < LANE // 2, moved_halo[1, axis, :, :LANE], moved_halo[0, axis, :, :LANE]
        )
    for side in range(2):
        moved_row_copy(side).start()
    for side in range(2):
        moved_row_copy(side).wait_recv()
    lower = lax.broadcasted_iota(jnp.int32, (SUB, width), 0) < HALO
    transports = [
        jnp.concatenate([moved[axis], jnp.where(lower, moved_halo[3, axis], moved_halo[2, axis])], axis=0)
        for axis in range(2)
    ]

    corner = flat[2]
    diagonal_inverse = flat[3]
    ocean = flat[4]
    face_x = ocean * east(ocean) * (east(transports[0]) - transports[0])
    face_y = ocean * north(ocean) * (north(transports[1]) - transports[1])
    spread = 0.5 * ((face_x + west(face_x)) + (face_y + south(face_y)))
    residual = flat[5] - (DIVERGE * ocean) * spread
    opening, updates = chebyshev_weights(ITERS)
    direction = opening * (residual * diagonal_inverse)
    surface = flat[1]
    for index in range(ITERS):
        surface = surface + direction
        if index + 1 < ITERS:
            residual = residual - operator(direction, corner)
            keep, push = updates[index]
            direction = keep * direction + push * (residual * diagonal_inverse)
    surface_out[...] = surface[:rows, :cols]

    for field in range(FIELDS):
        for tile in range(tiles):
            for group in range(groups):
                out_copy(group, field, tile, block if group < groups - 1 else last_count).wait()
    for side in range(2):
        pack_copy(side).wait_send()
        corner_copy(side).wait_send()
        moved_column_copy(side).wait_send()
        moved_row_copy(side).wait_send()
        row_copy(flat_group, 1, side).wait_send()

    def drain(group, carry):
        for side in range(2):
            row_copy(group, FIELDS, side).wait_send()
        return carry

    lax.fori_loop(0, groups, drain, 0)


def body(by_count, bx_count, u, v, t, s, wind, ssh, depth):
    levels, rows, cols = u.shape
    groups = -(-levels // SUB)
    span = rows + 2 * HALO
    width = cols + LANE
    f32 = jnp.float32
    flat_shape = (levels * rows, cols)
    args = [item.reshape(flat_shape) for item in (u, v, t, s)]
    outs = pl.pallas_call(
        functools.partial(kernel, levels, rows * by_count, by_count, bx_count),
        out_shape=[jax.ShapeDtypeStruct(flat_shape, f32)] * FIELDS + [jax.ShapeDtypeStruct(ssh.shape, f32)],
        in_specs=[pl.BlockSpec(memory_space=pl.ANY)] * FIELDS + [pl.BlockSpec(memory_space=pltpu.VMEM)] * 3,
        out_specs=[pl.BlockSpec(memory_space=pl.ANY)] * FIELDS + [pl.BlockSpec(memory_space=pltpu.VMEM)],
        scratch_shapes=[
            pltpu.VMEM((FIELDS, cols // LANE, (groups + 1) * SUB * rows, LANE), f32),
            pltpu.VMEM((groups + 1, FIELDS, span, SUB, width), f32),
            pltpu.VMEM((2, groups + 1, SUB, LANE), f32),
            pltpu.VMEM((2, groups + 1, SUB, LANE), f32),
            pltpu.VMEM((2, groups + 1, SUB, LANE), f32),
            pltpu.VMEM((2, groups + 1, SUB, LANE), f32),
            pltpu.VMEM((groups + 1, FIELDS, SUB, LANE), f32),
            pltpu.VMEM((FIELDS, span, SUB, width), f32),
            pltpu.VMEM((FIELDS, span, SUB, width), f32),
            pltpu.VMEM((span, SUB, width), f32),
            pltpu.VMEM((FIELDS, span, SUB, width), f32),
            pltpu.VMEM((SUB, LANE), f32),
            pltpu.VMEM((span, SUB, width), f32),
            pltpu.VMEM((span, SUB, width), f32),
            pltpu.VMEM((span, SUB, width), f32),
            pltpu.VMEM((span, SUB, width), f32),
            pltpu.VMEM((span, SUB, width), f32),
            pltpu.VMEM((2, span, SUB, width), f32),
            pltpu.VMEM((span, SUB, width), f32),
            pltpu.VMEM((2, rows, SUB, cols), f32),
            pltpu.VMEM((2, rows, width), f32),
            pltpu.VMEM((4, 2, rows, width), f32),
            pltpu.VMEM((6, span, width), f32),
            pltpu.SemaphoreType.DMA((FIELDS, cols // LANE)),
            pltpu.SemaphoreType.DMA((FIELDS, cols // LANE)),
            pltpu.SemaphoreType.DMA((2, groups + 1)),
            pltpu.SemaphoreType.DMA((2, groups + 1)),
            pltpu.SemaphoreType.DMA((2,)),
            pltpu.SemaphoreType.DMA((2,)),
            pltpu.SemaphoreType.DMA((2,)),
            pltpu.SemaphoreType.DMA((2,)),
            pltpu.SemaphoreType.DMA((4,)),
            pltpu.SemaphoreType.DMA((4,)),
        ],
        compiler_params=pltpu.CompilerParams(
            collective_id=0, has_side_effects=True, vmem_limit_bytes=40 << 20
        ),
    )(*args, wind.reshape(2 * rows, cols), ssh, depth)
    return tuple(item.reshape(u.shape) for item in outs[:FIELDS]) + (outs[FIELDS],)


def solution(mesh):
    whole = P(None, "by", "bx")
    flat = P("by", "bx")
    return jax.shard_map(
        functools.partial(body, mesh.shape["by"], mesh.shape["bx"]),
        mesh=mesh,
        in_specs=(whole,) * 5 + (flat, flat),
        out_specs=(whole,) * 4 + (flat,),
        check_vma=False,
    )
```

time: 328 us -> 76.6 us (0.23)
  the two profiles are of different devices: /device:TPU:6 before, /device:TPU:0 now
where the time goes in v1:
time: 76.6 us; the launch traced here: 76.2 us
  Pallas kernels  65.6 us (86%)
  local copies, waits for them, and re-layouts  9.98 us (13%)
    pallas_call x1, Pallas kernels, body(): pl.pallas_call(functools.partial(kernel, levels, rows * by_count, by_coun...  65.6 us
    unnamed x19, local copies, waits for them, and re-layouts  9.98 us

profile of v1, /device:TPU:0, one launch (start us, length us, event | category | flops | bytes accessed | tf_op | source)
XLA Modules:
  0.0 76.2 jit_solution(3134434580812597417)
XLA Ops:
  0.6 0.0 copy-start.5
  0.6 0.7 copy-done.5
  1.3 0.0 copy-start
  1.3 1.0 %copy-done = f32[62,8,256]{2,1,0:T(8,128)S(1)} copy-done((f32[62,8,256]{2,1,0:T(8,128)S(1)}, f32[62,8,256]{2,1,0:T(8,128)}, u32[]{:S(2)}) %copy-start) | copy-done | bytes 507928
  2.4 0.0 copy-start.1
  2.4 1.0 %copy-done.1 = f32[62,8,256]{2,1,0:T(8,128)S(1)} copy-done((f32[62,8,256]{2,1,0:T(8,128)S(1)}, f32[62,8,256]{2,1,0:T(8,128)}, u32[]{:S(2)}) %copy-start.1) | copy-done | bytes 507928
  3.4 0.0 copy-start.2
  3.4 1.0 %copy-done.2 = f32[62,8,256]{2,1,0:T(8,128)S(1)} copy-done((f32[62,8,256]{2,1,0:T(8,128)S(1)}, f32[62,8,256]{2,1,0:T(8,128)}, u32[]{:S(2)}) %copy-start.2) | copy-done | bytes 507928
  4.4 0.0 copy-start.3
  4.4 1.0 %copy-done.3 = f32[62,8,256]{2,1,0:T(8,128)S(1)} copy-done((f32[62,8,256]{2,1,0:T(8,128)S(1)}, f32[62,8,256]{2,1,0:T(8,128)}, u32[]{:S(2)}) %copy-start.3) | copy-done | bytes 507928
  5.5 0.0 copy-start.4
  5.5 0.7 copy-done.4
  6.2 0.0 copy-start.6
  6.2 0.7 copy-done.6
  6.9 65.6 %shard_map.110 = (f32[496,256]{1,0:T(8,128)S(1)}, f32[496,256]{1,0:T(8,128)S(1)}, f32[496,256]{1,0:T(8,128)S(1)}, f32[496,256]{1,0:T(8,128)S(1)}, f32[8,256]{1,0:T(8,128)S(1)}) custom-call(f32[496,256]{1,0:T(8,128)S(1)} %bitcast.13, f32[496,256]{1,0:T(8,128)S(1)} %bitcast.14, f32[496,256]{1,0:T(8,128)S(1)} %bitcast.15, f32[496,256]{1,0:T(8,128)S(1)} %bitcast.16, ...), custom_call_target="tpu_custom_call" | custom-call | tf_op jit(solution)/shard_map/pallas_call | solution.py:524
  72.5 0.8 %copy.17 = f32[62,8,256]{2,1,0:T(8,128)} copy(f32[62,8,256]{2,1,0:T(8,128)S(1)} %bitcast.12) | data formatting | bytes 1015808
  73.3 0.8 %copy.18 = f32[62,8,256]{2,1,0:T(8,128)} copy(f32[62,8,256]{2,1,0:T(8,128)S(1)} %bitcast.11) | data formatting | bytes 1015808
  74.0 0.8 %copy.19 = f32[62,8,256]{2,1,0:T(8,128)} copy(f32[62,8,256]{2,1,0:T(8,128)S(1)} %bitcast.10) | data formatting | bytes 1015808
  74.8 0.8 %copy.20 = f32[62,8,256]{2,1,0:T(8,128)} copy(f32[62,8,256]{2,1,0:T(8,128)S(1)} %bitcast.9) | data formatting | bytes 1015808
  75.6 0.6 copy.21
Async XLA Ops:
  0.6 0.7 copy-start.5
  1.3 1.0 %copy-start = (f32[62,8,256]{2,1,0:T(8,128)S(1)}, f32[62,8,256]{2,1,0:T(8,128)}, u32[]{:S(2)}) copy-start(f32[62,8,256]{2,1,0:T(8,128)} %param.7) | copy-start | bytes 1523716
  2.4 1.0 %copy-start.1 = (f32[62,8,256]{2,1,0:T(8,128)S(1)}, f32[62,8,256]{2,1,0:T(8,128)}, u32[]{:S(2)}) copy-start(f32[62,8,256]{2,1,0:T(8,128)} %param.8) | copy-start | bytes 1523716
  3.4 1.0 %copy-start.2 = (f32[62,8,256]{2,1,0:T(8,128)S(1)}, f32[62,8,256]{2,1,0:T(8,128)}, u32[]{:S(2)}) copy-start(f32[62,8,256]{2,1,0:T(8,128)} %param.9) | copy-start | bytes 1523716
  4.4 1.0 %copy-start.3 = (f32[62,8,256]{2,1,0:T(8,128)S(1)}, f32[62,8,256]{2,1,0:T(8,128)}, u32[]{:S(2)}) copy-start(f32[62,8,256]{2,1,0:T(8,128)} %param.10) | copy-start | bytes 1523716
  5.5 0.7 copy-start.4
  6.2 0.7 copy-start.6

commit v2 on v1

v2 whole, which is shorter than its diff:
```python
import functools
import math

import jax
import jax.numpy as jnp
from jax import lax
from jax.experimental import pallas as pl
from jax.experimental.pallas import tpu as pltpu
from jax.sharding import PartitionSpec as P

ITERS = 4
KAPPA = 0.004
ADVECT = 0.25
PRESS = 0.1
WIND = 0.5
PHI = 0.5
DIVERGE = 2.0
LOWER = 0.2
UPPER = 2.0

MESH = pl.DeviceIdType.MESH
FIELDS = 4
HALO = 4
SUB = 8
LANE = 128
AHEAD = 3
FIRST = 5
SECOND = 4
FINISH = 4


def chebyshev_weights(count):
    middle = 0.5 * (UPPER + LOWER)
    half_span = 0.5 * (UPPER - LOWER)
    ratio_value = middle / half_span
    rho_now = 1.0 / ratio_value
    updates = []
    for _ in range(count - 1):
        rho_next = 1.0 / (2.0 * ratio_value - rho_now)
        updates.append((rho_next * rho_now, 2.0 * rho_next / half_span))
        rho_now = rho_next
    return 1.0 / middle, updates


def east(x):
    return pltpu.roll(x, x.shape[1] - 1, 1)


def west(x):
    return pltpu.roll(x, 1, 1)


def north(x):
    return pltpu.roll(x, x.shape[0] - 1, 0)


def south(x):
    return pltpu.roll(x, 1, 0)


def slot_lane(field, row):
    return (field % 2) * 64 + row * 8 + (field // 2) * 4


def turn(x, shift):
    shift = shift % LANE
    return x if shift == 0 else pltpu.roll(x, shift, 1)


def kernel(
    levels, total_rows, by_count, bx_count,
    u_in, v_in, t_in, s_in, wind_in, ssh_in, depth_in,
    own, surface_out,
    ext, depth_own, pack_send, pack_recv, corner_send, corner_recv, edge,
    lap, mix, press, depth_c, depth_e, depth_n, stress, cor,
    flow_sum, moved, moved_rows, moved_cols, moved_corners, flat,
    in_sem, row_send, row_recv, pack_ss, pack_rs, corner_ss, corner_rs, moved_ss, moved_rs,
):
    inputs = (u_in, v_in, t_in, s_in)
    rows = SUB
    span = rows + 2 * HALO
    width = ext.shape[-1]
    cols = width - LANE
    tiles = cols // LANE
    groups = -(-levels // SUB)
    block = SUB * rows
    base = groups * block
    by = lax.axis_index("by")
    bx = lax.axis_index("bx")

    def device(step_y, step_x):
        return (lax.rem(by + step_y + by_count, by_count), lax.rem(bx + step_x + bx_count, bx_count))

    neighbours = [(y, x) for y in (-1, 0, 1) for x in (-1, 0, 1) if (y, x) != (0, 0)]

    def load_copies():
        result = []
        for tile in range(tiles):
            lanes = pl.ds(tile * LANE, LANE)
            for field in range(FIELDS):
                result.append(pltpu.make_async_copy(
                    inputs[field].at[:, lanes], own.at[field, tile, pl.ds(0, levels * rows)], in_sem.at[tile, field]
                ))
            result.append(pltpu.make_async_copy(
                ssh_in.at[:, lanes], own.at[0, tile, pl.ds(base + rows, rows)], in_sem.at[tile, FIELDS]
            ))
            result.append(pltpu.make_async_copy(
                wind_in.at[:, lanes], own.at[0, tile, pl.ds(base + 2 * rows, 2 * rows)], in_sem.at[tile, FIELDS + 1]
            ))
        result.append(pltpu.make_async_copy(depth_in, depth_own, in_sem.at[0, FIELDS + 2]))
        return result

    for copy in load_copies():
        copy.start()

    barrier = pltpu.get_barrier_semaphore()
    for step in neighbours:
        pl.semaphore_signal(barrier, inc=1, device_id=device(*step), device_id_type=MESH)

    lane = lax.broadcasted_iota(jnp.int32, (SUB, LANE), 1)
    for tile in range(tiles):
        for field in range(FIELDS):
            if levels % SUB:
                pad = base - levels * rows
                own[field, tile, levels * rows : base, :] = jnp.zeros((pad, LANE), jnp.float32)
        own[0, tile, base + 4 * rows : base + block, :] = jnp.zeros((block - 4 * rows, LANE), jnp.float32)

    def row_copy(group, fields, side):
        source = HALO + rows - HALO if side == 0 else HALO
        target = 0 if side == 0 else HALO + rows
        return pltpu.make_async_remote_copy(
            src_ref=ext.at[group, pl.ds(0, fields), pl.ds(source, HALO), :, pl.ds(0, cols)],
            dst_ref=ext.at[group, pl.ds(0, fields), pl.ds(target, HALO), :, pl.ds(0, cols)],
            send_sem=row_send.at[side, group],
            recv_sem=row_recv.at[side, group],
            device_id=device(1 - 2 * side, 0),
            device_id_type=MESH,
        )

    def pack_copy(side):
        return pltpu.make_async_remote_copy(
            src_ref=pack_send.at[side],
            dst_ref=pack_recv.at[1 - side],
            send_sem=pack_ss.at[side],
            recv_sem=pack_rs.at[1 - side],
            device_id=device(0, 2 * side - 1),
            device_id_type=MESH,
        )

    def corner_copy(side):
        return pltpu.make_async_remote_copy(
            src_ref=corner_send.at[side],
            dst_ref=corner_recv.at[side],
            send_sem=corner_ss.at[side],
            recv_sem=corner_rs.at[side],
            device_id=device(1 - 2 * side, 0),
            device_id_type=MESH,
        )

    def group_of(index):
        return lax.rem(index + groups, groups + 1)

    for copy in load_copies():
        copy.wait()
    for tile in range(tiles):
        own[0, tile, base : base + rows, :] = depth_own[:, tile * LANE : (tile + 1) * LANE].astype(jnp.float32)
    pl.semaphore_wait(barrier, len(neighbours))

    def stage_step(index, carry):
        group = group_of(index)
        west_pack = jnp.zeros((SUB, LANE), jnp.float32)
        east_pack = jnp.zeros((SUB, LANE), jnp.float32)
        for field in range(FIELDS):
            for row in range(rows):
                parts = [
                    own[field, tile, pl.ds(group * block + row, SUB, stride=rows), :]
                    for tile in range(tiles)
                ]
                for tile in range(tiles):
                    ext[group, field, HALO + row, :, tile * LANE : (tile + 1) * LANE] = parts[tile]
                first = slot_lane(field, row)
                here = (lane >= first) & (lane < first + HALO)
                west_pack = jnp.where(here, turn(parts[0], first), west_pack)
                east_pack = jnp.where(here, turn(parts[-1], first + HALO), east_pack)
        pack_send[0, group] = west_pack
        pack_send[1, group] = east_pack

        @pl.when(index == 0)
        def _():
            for side in range(2):
                row_copy(groups, 1, side).start()

        @pl.when(index == 1)
        def _():
            for side in range(2):
                row_copy(group, FIELDS, side).start()

        return carry

    lax.fori_loop(0, groups + 1, stage_step, 0)
    for side in range(2):
        pack_copy(side).start()

    row_index = by * rows - HALO + lax.broadcasted_iota(jnp.int32, (span, LANE), 0)
    turning = 1.2 * jnp.sin(0.9 * math.pi * ((row_index.astype(jnp.float32) + 0.5) / total_rows - 0.5))
    for row in range(span):
        cor[row] = jnp.broadcast_to(turning[row : row + 1, :], (SUB, LANE))

    for side in range(2):
        pack_copy(1 - side).wait_recv()
    own_lanes = (lane >= HALO * 8) & (lane < (HALO + rows) * 8)
    west_lanes = (lane & 7) < HALO

    def expand_step(group, carry):
        from_west = pack_recv[0, group]
        from_east = pack_recv[1, group]
        for_north = jnp.zeros((SUB, LANE), jnp.float32)
        for_south = jnp.zeros((SUB, LANE), jnp.float32)
        for field in range(FIELDS):
            shift = HALO * 8 - slot_lane(field, 0)
            both = jnp.where(west_lanes, turn(from_west, shift), turn(from_east, shift + HALO))
            edge[group, field] = both
            part = (lane >= field * 32) & (lane < field * 32 + 32)
            for_north = jnp.where(part, turn(both, field * 32 - rows * 8), for_north)
            for_south = jnp.where(part, turn(both, field * 32 - HALO * 8), for_south)
        corner_send[0, group] = for_north
        corner_send[1, group] = for_south
        return carry

    lax.fori_loop(0, groups + 1, expand_step, 0)
    for side in range(2):
        corner_copy(side).start()

    def send_step(group, carry):
        for side in range(2):
            row_copy(group, FIELDS, side).start()
        return carry

    lax.fori_loop(1, AHEAD, send_step, 0)

    sub = lax.broadcasted_iota(jnp.int32, (SUB, width), 0)
    level = sub.astype(jnp.float32)
    zeros = jnp.zeros((SUB, width), jnp.float32)

    def clear_step(row, carry):
        press[0, row] = zeros
        press[1, row] = zeros
        return carry

    lax.fori_loop(0, span, clear_step, 0)
    for axis in range(2):
        for row in range(rows):
            flow_sum[axis, row] = jnp.zeros((SUB, cols), jnp.float32)

    for side in range(2):
        corner_copy(side).wait_recv()

    def operator(field, corner):
        north_field = north(field)
        total = field + north_field
        change = north_field - field
        flux_x = corner * (0.5 * (east(total) - total))
        flux_y = corner * (0.5 * (east(change) + change))
        along_x = flux_x + south(flux_x)
        along_y = flux_y + west(flux_y)
        return PHI * field - 0.5 * ((along_x - west(along_x)) + (along_y - south(along_y)))

    def flat_tables():
        def table_step(row, carry):
            index = by * rows + (row - HALO)
            inside = (index >= 0) & (index < total_rows)
            here = jnp.where(inside, jnp.broadcast_to(ext[groups, 0, row, 0:1, :], (SUB, width)), 0.0)
            depth_c[row] = here
            depth_e[row] = jnp.minimum(here, east(here))
            for axis in range(2):
                wind = jnp.broadcast_to(ext[groups, 0, row, 2 + axis : 3 + axis, :], (SUB, width))
                stress[axis, row] = jnp.where(sub == 0, WIND * wind, 0.0)
            place = lax.rem(row + span - HALO, span)
            flat[0, pl.ds(place, 1), :] = here[0:1, :]
            flat[1, pl.ds(place, 1), :] = ext[groups, 0, row, 1:2, :]
            return carry

        lax.fori_loop(0, span, table_step, 0)

        def face_step(row, carry):
            depth_n[row] = jnp.minimum(depth_c[row], depth_c[row + 1])
            return carry

        lax.fori_loop(0, span - 1, face_step, 0)
        depth = flat[0]
        ssh = flat[1]
        near = jnp.minimum(depth, east(depth))
        corner = jnp.minimum(near, north(near)) * (1.0 / levels)
        pair = corner + west(corner)
        ocean = jnp.where(depth > 0.0, 1.0, 0.0)
        flat[2] = corner
        flat[3] = 1.0 / (PHI + 0.5 * (pair + south(pair)))
        flat[4] = ocean
        flat[5] = ocean * (PHI * ssh) - operator(ssh, corner)

    def cut(mask, value):
        return jnp.where(mask, value, 0.0)

    def tendencies(group):
        number = level + (group * SUB).astype(jnp.float32)

        def stage_pass(part, carry):
            slot = jnp.where(part == 0, group, groups + part)
            after = groups + 1 + part

            def first_block(index, inner):
                row = 1 + 2 * part + index * FIRST
                wet = [number < depth_c[row + k] for k in range(FIRST)]
                wet_e = [number < depth_e[row + k] for k in range(FIRST)]
                wet_n = [number < depth_n[row - 1 + k] for k in range(FIRST + 1)]
                speed = [
                    [(-0.5 * ADVECT) * ext[slot, field, row + k] for field in range(2)] for k in range(FIRST)
                ]
                for field in range(FIELDS):
                    cells = [ext[slot, field, row - 1 + k] for k in range(FIRST + 2)]
                    faces = [cut(wet_n[k], cells[k + 1] - cells[k]) for k in range(FIRST + 1)]
                    for k in range(FIRST):
                        here = cells[k + 1]
                        face_e = cut(wet_e[k], east(here) - here)
                        face_w = west(face_e)
                        lap[field, row + k] = (face_e - face_w) + (faces[k + 1] - faces[k])
                        mix[field, row + k] = speed[k][0] * (face_e + face_w) + speed[k][1] * (
                            faces[k + 1] + faces[k]
                        )
                above = [
                    jnp.broadcast_to(press[part, row + k, SUB - 1 : SUB, :], (SUB, width)) for k in range(FIRST)
                ]
                for k in range(FIRST):
                    running = cut(
                        wet[k],
                        (-0.8 * PRESS) * ext[slot, 2, row + k] + (0.6 * PRESS) * ext[slot, 3, row + k],
                    )
                    for shift in (1, 2, 4):
                        running = running + jnp.where(sub >= shift, pltpu.roll(running, shift, 0), 0.0)
                    press[part, row + k] = above[k] + running
                return inner

            def second_block(index, inner):
                row = 2 + 2 * part + index * SECOND
                wet = [number < depth_c[row + k] for k in range(SECOND)]
                wet_e = [number < depth_e[row + k] for k in range(SECOND)]
                wet_n = [number < depth_n[row - 1 + k] for k in range(SECOND + 1)]
                cells = [press[part, row - 1 + k] for k in range(SECOND + 2)]
                faces = [cut(wet_n[k], cells[k + 1] - cells[k]) for k in range(SECOND + 1)]
                forced = []
                for k in range(SECOND):
                    here = cells[k + 1]
                    face_e = cut(wet_e[k], east(here) - here)
                    turned = jnp.concatenate([cor[row + k]] * (width // LANE), axis=1)
                    forced.append((
                        cut(wet[k], turned * ext[slot, 1, row + k]) - 0.5 * (face_e + west(face_e)),
                        cut(wet[k], -turned * ext[slot, 0, row + k]) - 0.5 * (faces[k + 1] + faces[k]),
                    ))
                results = []
                for field in range(FIELDS):
                    cells = [lap[field, row - 1 + k] for k in range(SECOND + 2)]
                    faces = [cut(wet_n[k], cells[k + 1] - cells[k]) for k in range(SECOND + 1)]
                    for k in range(SECOND):
                        here = cells[k + 1]
                        face_e = cut(wet_e[k], east(here) - here)
                        twice = (face_e - west(face_e)) + (faces[k + 1] - faces[k])
                        value = (ext[slot, field, row + k] + mix[field, row + k]) - KAPPA * twice
                        results.append((field, row + k, value + forced[k][field] if field < 2 else value))
                for field, place, value in results:
                    ext[after, field, place] = value
                return inner

            lax.fori_loop(0, (span - 2 - 4 * part + FIRST - 1) // FIRST, first_block, 0)
            lax.fori_loop(0, (span - 4 - 4 * part + SECOND - 1) // SECOND, second_block, 0)
            def wind_step(row, inner):
                for axis in range(2):
                    ext[after, axis, row] = ext[after, axis, row] + cut(number < depth_c[row], stress[axis, row])
                return inner

            @pl.when(group == 0)
            def _():
                lax.fori_loop(2 + 2 * part, span - 2 - 2 * part, wind_step, 0)

            return carry

        lax.fori_loop(0, 2, stage_pass, 0)

        def finish_block(index, carry):
            for k in range(FINISH):
                row = index * FINISH + k
                wet = (number < depth_c[row + HALO])[:, :cols]
                for field in range(FIELDS):
                    value = 0.5 * (
                        ext[group, field, row + HALO, :, :cols] + ext[groups + 2, field, row + HALO, :, :cols]
                    )
                    for tile in range(tiles):
                        own[field, tile, pl.ds(group * block + row, SUB, stride=rows), :] = value[
                            :, tile * LANE : (tile + 1) * LANE
                        ]
                    if field < 2:
                        flow_sum[field, row] = flow_sum[field, row] + cut(wet, value)
            return carry

        lax.fori_loop(0, rows // FINISH, finish_block, 0)

    def group_step(index, carry):
        group = group_of(index)

        @pl.when(index == 0)
        def _():
            for side in range(2):
                row_copy(groups, 1, side).wait_recv()

        @pl.when(index > 0)
        def _():
            for side in range(2):
                row_copy(group, FIELDS, side).wait_recv()

        @pl.when((index > 0) & (index <= groups - AHEAD))
        def _():
            for side in range(2):
                row_copy(group + AHEAD, FIELDS, side).start()

        from_south = corner_recv[0, group]
        from_north = corner_recv[1, group]
        for field in range(FIELDS):
            all_rows = jnp.where(
                own_lanes,
                edge[group, field],
                jnp.where(lane < HALO * 8, turn(from_south, -32 * field), turn(from_north, 96 - 32 * field)),
            )
            for row in range(span):
                ext[group, field, row, :, cols:width] = turn(all_rows, LANE - HALO - 8 * row)

        @pl.when(index == 0)
        def _():
            flat_tables()

        @pl.when(index > 0)
        def _():
            tendencies(group)

        return carry

    lax.fori_loop(0, groups + 1, group_step, 0)

    def total_step(row, carry):
        for axis in range(2):
            total = jnp.sum(flow_sum[axis, row], axis=0, keepdims=True) * (1.0 / levels)
            moved[axis, pl.ds(row, 1), :] = total
        return carry

    lax.fori_loop(0, rows, total_step, 0)

    def moved_copy(step):
        y, x = step
        place = neighbours.index(step)
        other = neighbours.index((-y, -x))
        if x == 0:
            source, target = moved, moved_rows.at[(1 - y) // 2]
        else:
            tile = tiles - 1 if x > 0 else 0
            source = moved.at[:, :, pl.ds(tile * LANE, LANE)]
            side = (1 - x) // 2
            target = moved_cols.at[side] if y == 0 else moved_corners.at[(1 - y) // 2, side]
        return pltpu.make_async_remote_copy(
            src_ref=source, dst_ref=target, send_sem=moved_ss.at[place], recv_sem=moved_rs.at[place],
            device_id=device(y, x), device_id_type=MESH,
        )

    for step in neighbours:
        moved_copy(step).start()
    for step in neighbours:
        moved_copy(step).wait_recv()
    lower = lax.broadcasted_iota(jnp.int32, (SUB, cols), 0) < HALO
    lower_tile = lax.broadcasted_iota(jnp.int32, (SUB, LANE), 0) < HALO
    right = lane < LANE // 2
    transports = []
    for axis in range(2):
        near = jnp.concatenate(
            [moved[axis], jnp.where(right, moved_cols[1, axis], moved_cols[0, axis])], axis=1
        )
        corners = [
            jnp.where(right, moved_corners[side, 1, axis], moved_corners[side, 0, axis]) for side in range(2)
        ]
        far = jnp.concatenate(
            [
                jnp.where(lower, moved_rows[1, axis], moved_rows[0, axis]),
                jnp.where(lower_tile, corners[1], corners[0]),
            ],
            axis=1,
        )
        transports.append(jnp.concatenate([near, far], axis=0))

    corner = flat[2]
    diagonal_inverse = flat[3]
    ocean = flat[4]
    face_x = ocean * east(ocean) * (east(transports[0]) - transports[0])
    face_y = ocean * north(ocean) * (north(transports[1]) - transports[1])
    spread = 0.5 * ((face_x + west(face_x)) + (face_y + south(face_y)))
    residual = flat[5] - (DIVERGE * ocean) * spread
    opening, updates = chebyshev_weights(ITERS)
    direction = opening * (residual * diagonal_inverse)

    def pick(index, values):
        result = jnp.float32(values[-1])
        for k in range(len(values) - 1):
            result = jnp.where(index == k, jnp.float32(values[k]), result)
        return result

    def solve_step(index, carry):
        surface, residual, direction = carry
        surface = surface + direction
        residual = residual - operator(direction, corner)
        keep = pick(index, [item[0] for item in updates])
        push = pick(index, [item[1] for item in updates])
        direction = keep * direction + push * (residual * diagonal_inverse)
        return surface, residual, direction

    surface, residual, direction = lax.fori_loop(0, ITERS - 1, solve_step, (flat[1], residual, direction))
    surface_out[...] = (surface + direction)[:rows, :cols]

    for side in range(2):
        pack_copy(side).wait_send()
        corner_copy(side).wait_send()
        row_copy(groups, 1, side).wait_send()
    for step in neighbours:
        moved_copy(step).wait_send()

    def drain(group, carry):
        for side in range(2):
            row_copy(group, FIELDS, side).wait_send()
        return carry

    lax.fori_loop(0, groups, drain, 0)


def deliver(levels, fields_in, surface_in, u_out, v_out, t_out, s_out, surface_out, sems):
    outputs = (u_out, v_out, t_out, s_out)
    count = u_out.shape[0]
    copies = [
        pltpu.make_async_copy(
            fields_in.at[field, tile, pl.ds(0, count)],
            outputs[field].at[:, pl.ds(tile * LANE, LANE)],
            sems.at[field, tile],
        )
        for field in range(FIELDS)
        for tile in range(fields_in.shape[1])
    ]
    copies.append(pltpu.make_async_copy(surface_in, surface_out, sems.at[FIELDS, 0]))
    for copy in copies:
        copy.start()
    for copy in copies:
        copy.wait()


def body(by_count, bx_count, u, v, t, s, wind, ssh, depth):
    levels, rows, cols = u.shape
    groups = -(-levels // SUB)
    span = rows + 2 * HALO
    room = span + 4
    tiles = cols // LANE
    width = cols + LANE
    f32 = jnp.float32
    flat_shape = (levels * rows, cols)
    args = [item.reshape(flat_shape) for item in (u, v, t, s)]
    own = jax.ShapeDtypeStruct((FIELDS, tiles, (groups + 1) * SUB * rows, LANE), f32)
    done, surface = pl.pallas_call(
        functools.partial(kernel, levels, rows * by_count, by_count, bx_count),
        out_shape=[own, jax.ShapeDtypeStruct(ssh.shape, f32)],
        in_specs=[pl.BlockSpec(memory_space=pltpu.HBM)] * (FIELDS + 3),
        out_specs=[pl.BlockSpec(memory_space=pltpu.VMEM)] * 2,
        scratch_shapes=[
            pltpu.VMEM((groups + 3, FIELDS, room, SUB, width), f32),
            pltpu.VMEM((rows, cols), jnp.int32),
            pltpu.VMEM((2, groups + 1, SUB, LANE), f32),
            pltpu.VMEM((2, groups + 1, SUB, LANE), f32),
            pltpu.VMEM((2, groups + 1, SUB, LANE), f32),
            pltpu.VMEM((2, groups + 1, SUB, LANE), f32),
            pltpu.VMEM((groups + 1, FIELDS, SUB, LANE), f32),
            pltpu.VMEM((FIELDS, room, SUB, width), f32),
            pltpu.VMEM((FIELDS, room, SUB, width), f32),
            pltpu.VMEM((2, room, SUB, width), f32),
            pltpu.VMEM((room, SUB, width), f32),
            pltpu.VMEM((room, SUB, width), f32),
            pltpu.VMEM((room, SUB, width), f32),
            pltpu.VMEM((2, room, SUB, width), f32),
            pltpu.VMEM((room, SUB, LANE), f32),
            pltpu.VMEM((2, rows, SUB, cols), f32),
            pltpu.VMEM((2, rows, cols), f32),
            pltpu.VMEM((2, 2, rows, cols), f32),
            pltpu.VMEM((2, 2, rows, LANE), f32),
            pltpu.VMEM((2, 2, 2, rows, LANE), f32),
            pltpu.VMEM((6, span, width), f32),
            pltpu.SemaphoreType.DMA((tiles, FIELDS + 3)),
            pltpu.SemaphoreType.DMA((2, groups + 1)),
            pltpu.SemaphoreType.DMA((2, groups + 1)),
            pltpu.SemaphoreType.DMA((2,)),
            pltpu.SemaphoreType.DMA((2,)),
            pltpu.SemaphoreType.DMA((2,)),
            pltpu.SemaphoreType.DMA((2,)),
            pltpu.SemaphoreType.DMA((8,)),
            pltpu.SemaphoreType.DMA((8,)),
        ],
        compiler_params=pltpu.CompilerParams(
            collective_id=0, has_side_effects=True, vmem_limit_bytes=61 << 20
        ),
    )(*args, wind.reshape(2 * rows, cols), ssh, depth)
    outs = pl.pallas_call(
        functools.partial(deliver, levels),
        out_shape=[jax.ShapeDtypeStruct(flat_shape, f32)] * FIELDS + [jax.ShapeDtypeStruct(ssh.shape, f32)],
        in_specs=[pl.BlockSpec(memory_space=pltpu.VMEM)] * 2,
        out_specs=[pl.BlockSpec(memory_space=pltpu.HBM)] * (FIELDS + 1),
        scratch_shapes=[pltpu.SemaphoreType.DMA((FIELDS + 1, tiles))],
    )(done, surface)
    return tuple(item.reshape(u.shape) for item in outs[:FIELDS]) + (outs[FIELDS],)


def solution(mesh):
    whole = P(None, "by", "bx")
    flat = P("by", "bx")
    return jax.shard_map(
        functools.partial(body, mesh.shape["by"], mesh.shape["bx"]),
        mesh=mesh,
        in_specs=(whole,) * 5 + (flat, flat),
        out_specs=(whole,) * 4 + (flat,),
        check_vma=False,
    )
```

time: 76.6 us -> 61.7 us (0.81)
  the two profiles are of different devices: /device:TPU:0 before, /device:TPU:1 now
where the time goes in v2:
time: 61.7 us; the launch traced here: 61.5 us
  Pallas kernels  60.9 us (99%)
  between operations  0.64 us (1%)
    pallas_call x1, Pallas kernels, body(): pl.pallas_call(functools.partial(kernel, levels, rows * by_count, by_coun...  57.8 us
    pallas_call x1, Pallas kernels, body(): pl.pallas_call(functools.partial(deliver, levels), out_shape=[jax.ShapeDt...  3.04 us

profile of v2, /device:TPU:1, one launch (start us, length us, event | category | flops | bytes accessed | tf_op | source)
XLA Modules:
  0.0 61.5 jit_solution(2635491049426855436)
XLA Ops:
  0.6 57.8 %shard_map.110 = (f32[4,2,576,128]{3,2,1,0:T(8,128)}, f32[8,256]{1,0:T(8,128)}) custom-call(f32[496,256]{1,0:T(8,128)} %bitcast.9, f32[496,256]{1,0:T(8,128)} %bitcast.10, f32[496,256]{1,0:T(8,128)} %bitcast.11, f32[496,256]{1,0:T(8,128)} %bitcast.12, f32[16,256]{1,0:T(8,128)} %bitcast.13, f32[8,256]{1,0:T(8,128)} %ssh_in.1, s32[8,256]{1,0:T(8,128)} %depth_in.1), custom_call_target="tpu_custom_call" | custom-call | tf_op jit(solution)/shard_map/pallas_call | solution.py:568
  58.5 3.0 %shard_map.111 = (f32[496,256]{1,0:T(8,128)}, f32[496,256]{1,0:T(8,128)}, f32[496,256]{1,0:T(8,128)}, f32[496,256]{1,0:T(8,128)}, f32[8,256]{1,0:T(8,128)}) custom-call(f32[4,2,576,128]{3,2,1,0:T(8,128)} %get-tuple-element.12.fields_in, f32[8,256]{1,0:T(8,128)} %get-tuple-element.13.surface_in), custom_call_target="tpu_custom_call" | custom-call | tf_op jit(solution)/shard_map/pallas_call | solution.py:609

commit v3 on v2

--- a/solution.py
+++ b/solution.py
@@ -23,10 +23,10 @@
 HALO = 4
 SUB = 8
 LANE = 128
-AHEAD = 3
+BATCH = 3
 FIRST = 5
 SECOND = 4
-FINISH = 4
+FINISH = 8
 
 
 def chebyshev_weights(count):
@@ -71,10 +71,10 @@
     levels, total_rows, by_count, bx_count,
     u_in, v_in, t_in, s_in, wind_in, ssh_in, depth_in,
     own, surface_out,
-    ext, depth_own, pack_send, pack_recv, corner_send, corner_recv, edge,
+    ext, depth_own, pack_send, pack_recv,
     lap, mix, press, depth_c, depth_e, depth_n, stress, cor,
     flow_sum, moved, moved_rows, moved_cols, moved_corners, flat,
-    in_sem, row_send, row_recv, pack_ss, pack_rs, corner_ss, corner_rs, moved_ss, moved_rs,
+    in_sem, row_send, row_recv, pack_ss, pack_rs, moved_ss, moved_rs,
 ):
     inputs = (u_in, v_in, t_in, s_in)
     rows = SUB
@@ -137,25 +137,21 @@
             device_id_type=MESH,
         )
 
-    def pack_copy(side):
+    batches = ((0, BATCH), (BATCH, groups + 1 - BATCH))
+
+    def pack_copy(batch, y, x):
+        first, count = batches[batch]
+        place = 2 * (y % 3) + (1 - x) // 2
         return pltpu.make_async_remote_copy(
-            src_ref=pack_send.at[side],
-            dst_ref=pack_recv.at[1 - side],
-            send_sem=pack_ss.at[side],
-            recv_sem=pack_rs.at[1 - side],
-            device_id=device(0, 2 * side - 1),
+            src_ref=pack_send.at[(1 + x) // 2, pl.ds(first, count)],
+            dst_ref=pack_recv.at[y % 3, (1 - x) // 2, pl.ds(first, count)],
+            send_sem=pack_ss.at[batch, place],
+            recv_sem=pack_rs.at[batch, place],
+            device_id=device(y, x),
             device_id_type=MESH,
         )
 
-    def corner_copy(side):
-        return pltpu.make_async_remote_copy(
-            src_ref=corner_send.at[side],
-            dst_ref=corner_recv.at[side],
-            send_sem=corner_ss.at[side],
-            recv_sem=corner_rs.at[side],
-            device_id=device(1 - 2 * side, 0),
-            device_id_type=MESH,
-        )
+    sideways = [(y, x) for y in (0, 1, -1) for x in (-1, 1)]
 
     def group_of(index):
         return lax.rem(index + groups, groups + 1)
@@ -182,78 +178,55 @@
                 here = (lane >= first) & (lane < first + HALO)
                 west_pack = jnp.where(here, turn(parts[0], first), west_pack)
                 east_pack = jnp.where(here, turn(parts[-1], first + HALO), east_pack)
-        pack_send[0, group] = west_pack
-        pack_send[1, group] = east_pack
+        pack_send[0, index] = west_pack
+        pack_send[1, index] = east_pack
+
+        return carry
+
+    assert (groups + 1) % BATCH == 0
+
+    def stage_batch(index, carry):
+        for k in range(BATCH):
+            stage_step(index * BATCH + k, 0)
 
         @pl.when(index == 0)
         def _():
             for side in range(2):
                 row_copy(groups, 1, side).start()
-
-        @pl.when(index == 1)
-        def _():
-            for side in range(2):
-                row_copy(group, FIELDS, side).start()
+            for step in sideways:
+                pack_copy(0, *step).start()
+            for group in range(BATCH - 1):
+                for side in range(2):
+                    row_copy(group, FIELDS, side).start()
 
         return carry
 
-    lax.fori_loop(0, groups + 1, stage_step, 0)
-    for side in range(2):
-        pack_copy(side).start()
+    lax.fori_loop(0, (groups + 1) // BATCH, stage_batch, 0)
+    for step in sideways:
+        pack_copy(1, *step).start()
+
+    def send_step(group, carry):
+        for side in range(2):
+            row_copy(group, FIELDS, side).start()
+        return carry
+
+    lax.fori_loop(BATCH - 1, groups, send_step, 0)
 
     row_index = by * rows - HALO + lax.broadcasted_iota(jnp.int32, (span, LANE), 0)
     turning = 1.2 * jnp.sin(0.9 * math.pi * ((row_index.astype(jnp.float32) + 0.5) / total_rows - 0.5))
     for row in range(span):
         cor[row] = jnp.broadcast_to(turning[row : row + 1, :], (SUB, LANE))
 
-    for side in range(2):
-        pack_copy(1 - side).wait_recv()
-    own_lanes = (lane >= HALO * 8) & (lane < (HALO + rows) * 8)
-    west_lanes = (lane & 7) < HALO
-
-    def expand_step(group, carry):
-        from_west = pack_recv[0, group]
-        from_east = pack_recv[1, group]
-        for_north = jnp.zeros((SUB, LANE), jnp.float32)
-        for_south = jnp.zeros((SUB, LANE), jnp.float32)
-        for field in range(FIELDS):
-            shift = HALO * 8 - slot_lane(field, 0)
-            both = jnp.where(west_lanes, turn(from_west, shift), turn(from_east, shift + HALO))
-            edge[group, field] = both
-            part = (lane >= field * 32) & (lane < field * 32 + 32)
-            for_north = jnp.where(part, turn(both, field * 32 - rows * 8), for_north)
-            for_south = jnp.where(part, turn(both, field * 32 - HALO * 8), for_south)
-        corner_send[0, group] = for_north
-        corner_send[1, group] = for_south
-        return carry
-
-    lax.fori_loop(0, groups + 1, expand_step, 0)
-    for side in range(2):
-        corner_copy(side).start()
-
-    def send_step(group, carry):
-        for side in range(2):
-            row_copy(group, FIELDS, side).start()
-        return carry
-
-    lax.fori_loop(1, AHEAD, send_step, 0)
-
     sub = lax.broadcasted_iota(jnp.int32, (SUB, width), 0)
     level = sub.astype(jnp.float32)
     zeros = jnp.zeros((SUB, width), jnp.float32)
 
-    def clear_step(row, carry):
+    for row in range(span):
         press[0, row] = zeros
         press[1, row] = zeros
-        return carry
-
-    lax.fori_loop(0, span, clear_step, 0)
     for axis in range(2):
         for row in range(rows):
             flow_sum[axis, row] = jnp.zeros((SUB, cols), jnp.float32)
-
-    for side in range(2):
-        corner_copy(side).wait_recv()
 
     def operator(field, corner):
         north_field = north(field)
@@ -266,27 +239,21 @@
         return PHI * field - 0.5 * ((along_x - west(along_x)) + (along_y - south(along_y)))
 
     def flat_tables():
-        def table_step(row, carry):
+        for row in range(span):
             index = by * rows + (row - HALO)
             inside = (index >= 0) & (index < total_rows)
             here = jnp.where(inside, jnp.broadcast_to(ext[groups, 0, row, 0:1, :], (SUB, width)), 0.0)
             depth_c[row] = here
             depth_e[row] = jnp.minimum(here, east(here))
+            if row > 0:
+                depth_n[row - 1] = jnp.minimum(before, here)
+            before = here
             for axis in range(2):
                 wind = jnp.broadcast_to(ext[groups, 0, row, 2 + axis : 3 + axis, :], (SUB, width))
                 stress[axis, row] = jnp.where(sub == 0, WIND * wind, 0.0)
-            place = lax.rem(row + span - HALO, span)
-            flat[0, pl.ds(place, 1), :] = here[0:1, :]
-            flat[1, pl.ds(place, 1), :] = ext[groups, 0, row, 1:2, :]
-            return carry
-
-        lax.fori_loop(0, span, table_step, 0)
-
-        def face_step(row, carry):
-            depth_n[row] = jnp.minimum(depth_c[row], depth_c[row + 1])
-            return carry
-
-        lax.fori_loop(0, span - 1, face_step, 0)
+            place = (row + span - HALO) % span
+            flat[0, place : place + 1, :] = here[0:1, :]
+            flat[1, place : place + 1, :] = ext[groups, 0, row, 1:2, :]
         depth = flat[0]
         ssh = flat[1]
         near = jnp.minimum(depth, east(depth))
@@ -372,14 +339,11 @@
 
             lax.fori_loop(0, (span - 2 - 4 * part + FIRST - 1) // FIRST, first_block, 0)
             lax.fori_loop(0, (span - 4 - 4 * part + SECOND - 1) // SECOND, second_block, 0)
-            def wind_step(row, inner):
-                for axis in range(2):
-                    ext[after, axis, row] = ext[after, axis, row] + cut(number < depth_c[row], stress[axis, row])
-                return inner
-
             @pl.when(group == 0)
             def _():
-                lax.fori_loop(2 + 2 * part, span - 2 - 2 * part, wind_step, 0)
+                for row in range(2, span - 2):
+                    for axis in range(2):
+                        ext[after, axis, row] = ext[after, axis, row] + cut(number < depth_c[row], stress[axis, row])
 
             return carry
 
@@ -403,54 +367,50 @@
 
         lax.fori_loop(0, rows // FINISH, finish_block, 0)
 
-    def group_step(index, carry):
-        group = group_of(index)
-
-        @pl.when(index == 0)
-        def _():
-            for side in range(2):
-                row_copy(groups, 1, side).wait_recv()
-
-        @pl.when(index > 0)
-        def _():
-            for side in range(2):
-                row_copy(group, FIELDS, side).wait_recv()
-
-        @pl.when((index > 0) & (index <= groups - AHEAD))
-        def _():
-            for side in range(2):
-                row_copy(group + AHEAD, FIELDS, side).start()
-
-        from_south = corner_recv[0, group]
-        from_north = corner_recv[1, group]
-        for field in range(FIELDS):
+    west_lanes = (lane & 7) < HALO
+
+    def widen(index, group, fields):
+        packs = [[pack_recv[y, x, index] for x in range(2)] for y in range(3)]
+        for field in range(fields):
+            shifts = (
+                HALO * 8 - slot_lane(field, 0), -slot_lane(field, rows - HALO), (HALO + rows) * 8 - slot_lane(field, 0)
+            )
+            parts = [
+                jnp.where(west_lanes, turn(packs[y][0], shifts[y]), turn(packs[y][1], shifts[y] + HALO))
+                for y in range(3)
+            ]
             all_rows = jnp.where(
-                own_lanes,
-                edge[group, field],
-                jnp.where(lane < HALO * 8, turn(from_south, -32 * field), turn(from_north, 96 - 32 * field)),
+                lane < HALO * 8, parts[1], jnp.where(lane < (HALO + rows) * 8, parts[0], parts[2])
             )
             for row in range(span):
                 ext[group, field, row, :, cols:width] = turn(all_rows, LANE - HALO - 8 * row)
 
-        @pl.when(index == 0)
+    for step in sideways:
+        pack_copy(0, *step).wait_recv()
+    for side in range(2):
+        row_copy(groups, 1, side).wait_recv()
+    widen(0, groups, 1)
+    flat_tables()
+
+    def group_step(group, carry):
+        for side in range(2):
+            row_copy(group, FIELDS, side).wait_recv()
+
+        @pl.when(group == BATCH - 1)
         def _():
-            flat_tables()
-
-        @pl.when(index > 0)
-        def _():
-            tendencies(group)
-
+            for step in sideways:
+                pack_copy(1, *step).wait_recv()
+
+        widen(group + 1, group, FIELDS)
+        tendencies(group)
         return carry
 
-    lax.fori_loop(0, groups + 1, group_step, 0)
-
-    def total_step(row, carry):
+    lax.fori_loop(0, groups, group_step, 0)
+
+    for row in range(rows):
         for axis in range(2):
             total = jnp.sum(flow_sum[axis, row], axis=0, keepdims=True) * (1.0 / levels)
-            moved[axis, pl.ds(row, 1), :] = total
-        return carry
-
-    lax.fori_loop(0, rows, total_step, 0)
+            moved[axis, row : row + 1, :] = total
 
     def moved_copy(step):
         y, x = step
@@ -521,11 +481,12 @@
     surface_out[...] = (surface + direction)[:rows, :cols]
 
     for side in range(2):
-        pack_copy(side).wait_send()
-        corner_copy(side).wait_send()
         row_copy(groups, 1, side).wait_send()
     for step in neighbours:
         moved_copy(step).wait_send()
+    for step in sideways:
+        for batch in range(2):
+            pack_copy(batch, *step).wait_send()
 
     def drain(group, carry):
         for side in range(2):
@@ -567,17 +528,14 @@
     own = jax.ShapeDtypeStruct((FIELDS, tiles, (groups + 1) * SUB * rows, LANE), f32)
     done, surface = pl.pallas_call(
         functools.partial(kernel, levels, rows * by_count, by_count, bx_count),
-        out_shape=[own, jax.ShapeDtypeStruct(ssh.shape, f32)],
+        out_shape=[pltpu.VMEM(own.shape, f32), pltpu.VMEM(ssh.shape, f32)],
         in_specs=[pl.BlockSpec(memory_space=pltpu.HBM)] * (FIELDS + 3),
         out_specs=[pl.BlockSpec(memory_space=pltpu.VMEM)] * 2,
         scratch_shapes=[
             pltpu.VMEM((groups + 3, FIELDS, room, SUB, width), f32),
             pltpu.VMEM((rows, cols), jnp.int32),
             pltpu.VMEM((2, groups + 1, SUB, LANE), f32),
-            pltpu.VMEM((2, groups + 1, SUB, LANE), f32),
-            pltpu.VMEM((2, groups + 1, SUB, LANE), f32),
-            pltpu.VMEM((2, groups + 1, SUB, LANE), f32),
-            pltpu.VMEM((groups + 1, FIELDS, SUB, LANE), f32),
+            pltpu.VMEM((3, 2, groups + 1, SUB, LANE), f32),
             pltpu.VMEM((FIELDS, room, SUB, width), f32),
             pltpu.VMEM((FIELDS, room, SUB, width), f32),
             pltpu.VMEM((2, room, SUB, width), f32),
@@ -595,10 +553,8 @@
             pltpu.SemaphoreType.DMA((tiles, FIELDS + 3)),
             pltpu.SemaphoreType.DMA((2, groups + 1)),
             pltpu.SemaphoreType.DMA((2, groups + 1)),
-            pltpu.SemaphoreType.DMA((2,)),
-            pltpu.SemaphoreType.DMA((2,)),
-            pltpu.SemaphoreType.DMA((2,)),
-            pltpu.SemaphoreType.DMA((2,)),
+            pltpu.SemaphoreType.DMA((2, 6)),
+            pltpu.SemaphoreType.DMA((2, 6)),
             pltpu.SemaphoreType.DMA((8,)),
             pltpu.SemaphoreType.DMA((8,)),
         ],
@@ -612,6 +568,7 @@
         in_specs=[pl.BlockSpec(memory_space=pltpu.VMEM)] * 2,
         out_specs=[pl.BlockSpec(memory_space=pltpu.HBM)] * (FIELDS + 1),
         scratch_shapes=[pltpu.SemaphoreType.DMA((FIELDS + 1, tiles))],
+        compiler_params=pltpu.CompilerParams(vmem_limit_bytes=4 << 20),
     )(done, surface)
     return tuple(item.reshape(u.shape) for item in outs[:FIELDS]) + (outs[FIELDS],)
 

time: 61.7 us -> 53.7 us (0.87)
  Pallas kernels: 60.9 us -> 52.9 us
    pallas_call x1, Pallas kernels: 57.8 us -> 51.5 us  [body(): pl.pallas_call(functools.partial(kernel, levels, rows * by_count, by_coun...]
    pallas_call x1, Pallas kernels: 3.04 us -> 1.37 us  [body(): pl.pallas_call(functools.partial(deliver, levels), out_shape=[jax.ShapeDt...]
where the time goes in v3:
time: 53.7 us; the launch traced here: 53.5 us
  Pallas kernels  52.9 us (99%)
  between operations  0.64 us (1%)
    pallas_call x1, Pallas kernels, body(): pl.pallas_call(functools.partial(kernel, levels, rows * by_count, by_coun...  51.5 us
    pallas_call x1, Pallas kernels, body(): pl.pallas_call(functools.partial(deliver, levels), out_shape=[jax.ShapeDt...  1.37 us

profile of v3, /device:TPU:1, one launch (start us, length us, event | category | flops | bytes accessed | tf_op | source)
XLA Modules:
  0.0 53.5 jit_solution(17665100001263006628)
XLA Ops:
  0.6 51.5 %shard_map.110 = (f32[4,2,576,128]{3,2,1,0:T(8,128)S(1)}, f32[8,256]{1,0:T(8,128)S(1)}) custom-call(f32[496,256]{1,0:T(8,128)} %bitcast.9, f32[496,256]{1,0:T(8,128)} %bitcast.10, f32[496,256]{1,0:T(8,128)} %bitcast.11, f32[496,256]{1,0:T(8,128)} %bitcast.12, f32[16,256]{1,0:T(8,128)} %bitcast.13, f32[8,256]{1,0:T(8,128)} %ssh_in.1, s32[8,256]{1,0:T(8,128)} %depth_in.1), custom_call_target="tpu_custom_call" | custom-call | tf_op jit(solution)/shard_map/pallas_call | solution.py:529
  52.1 1.4 %shard_map.111 = (f32[496,256]{1,0:T(8,128)}, f32[496,256]{1,0:T(8,128)}, f32[496,256]{1,0:T(8,128)}, f32[496,256]{1,0:T(8,128)}, f32[8,256]{1,0:T(8,128)}) custom-call(f32[4,2,576,128]{3,2,1,0:T(8,128)S(1)} %get-tuple-element.12.fields_in, f32[8,256]{1,0:T(8,128)S(1)} %get-tuple-element.13.surface_in), custom_call_target="tpu_custom_call" | custom-call | tf_op jit(solution)/shard_map/pallas_call | solution.py:565

commit v4 on v3

--- a/solution.py
+++ b/solution.py
@@ -23,10 +23,9 @@
 HALO = 4
 SUB = 8
 LANE = 128
-BATCH = 3
+BATCH = 4
 FIRST = 5
 SECOND = 4
-FINISH = 8
 
 
 def chebyshev_weights(count):
@@ -84,7 +83,8 @@
     tiles = cols // LANE
     groups = -(-levels // SUB)
     block = SUB * rows
-    base = groups * block
+    lead = groups * SUB - levels
+    assert lead >= 2
     by = lax.axis_index("by")
     bx = lax.axis_index("bx")
 
@@ -99,13 +99,13 @@
             lanes = pl.ds(tile * LANE, LANE)
             for field in range(FIELDS):
                 result.append(pltpu.make_async_copy(
-                    inputs[field].at[:, lanes], own.at[field, tile, pl.ds(0, levels * rows)], in_sem.at[tile, field]
+                    inputs[field].at[:, lanes], own.at[field, tile, pl.ds(lead * rows, levels * rows)], in_sem.at[tile, field]
                 ))
             result.append(pltpu.make_async_copy(
-                ssh_in.at[:, lanes], own.at[0, tile, pl.ds(base + rows, rows)], in_sem.at[tile, FIELDS]
+                ssh_in.at[:, lanes], own.at[0, tile, pl.ds(rows, rows)], in_sem.at[tile, FIELDS]
             ))
             result.append(pltpu.make_async_copy(
-                wind_in.at[:, lanes], own.at[0, tile, pl.ds(base + 2 * rows, 2 * rows)], in_sem.at[tile, FIELDS + 1]
+                wind_in.at[:, lanes], own.at[1, tile, pl.ds(0, 2 * rows)], in_sem.at[tile, FIELDS + 1]
             ))
         result.append(pltpu.make_async_copy(depth_in, depth_own, in_sem.at[0, FIELDS + 2]))
         return result
@@ -119,25 +119,25 @@
 
     lane = lax.broadcasted_iota(jnp.int32, (SUB, LANE), 1)
     for tile in range(tiles):
-        for field in range(FIELDS):
-            if levels % SUB:
-                pad = base - levels * rows
-                own[field, tile, levels * rows : base, :] = jnp.zeros((pad, LANE), jnp.float32)
-        own[0, tile, base + 4 * rows : base + block, :] = jnp.zeros((block - 4 * rows, LANE), jnp.float32)
-
-    def row_copy(group, fields, side):
+        for field in range(2, FIELDS):
+            own[field, tile, : lead * rows, :] = jnp.zeros((lead * rows, LANE), jnp.float32)
+        if lead > 2:
+            for field in range(2):
+                own[field, tile, 2 * rows : lead * rows, :] = jnp.zeros(((lead - 2) * rows, LANE), jnp.float32)
+
+    def row_copy(group, side):
         source = HALO + rows - HALO if side == 0 else HALO
         target = 0 if side == 0 else HALO + rows
         return pltpu.make_async_remote_copy(
-            src_ref=ext.at[group, pl.ds(0, fields), pl.ds(source, HALO), :, pl.ds(0, cols)],
-            dst_ref=ext.at[group, pl.ds(0, fields), pl.ds(target, HALO), :, pl.ds(0, cols)],
+            src_ref=ext.at[group, :, pl.ds(source, HALO), :, pl.ds(0, cols)],
+            dst_ref=ext.at[group, :, pl.ds(target, HALO), :, pl.ds(0, cols)],
             send_sem=row_send.at[side, group],
             recv_sem=row_recv.at[side, group],
             device_id=device(1 - 2 * side, 0),
             device_id_type=MESH,
         )
 
-    batches = ((0, BATCH), (BATCH, groups + 1 - BATCH))
+    batches = ((0, BATCH), (BATCH, groups - BATCH))
 
     def pack_copy(batch, y, x):
         first, count = batches[batch]
@@ -153,17 +153,13 @@
 
     sideways = [(y, x) for y in (0, 1, -1) for x in (-1, 1)]
 
-    def group_of(index):
-        return lax.rem(index + groups, groups + 1)
-
     for copy in load_copies():
         copy.wait()
     for tile in range(tiles):
-        own[0, tile, base : base + rows, :] = depth_own[:, tile * LANE : (tile + 1) * LANE].astype(jnp.float32)
+        own[0, tile, :rows, :] = depth_own[:, tile * LANE : (tile + 1) * LANE].astype(jnp.float32)
     pl.semaphore_wait(barrier, len(neighbours))
 
-    def stage_step(index, carry):
-        group = group_of(index)
+    def stage_step(group):
         west_pack = jnp.zeros((SUB, LANE), jnp.float32)
         east_pack = jnp.zeros((SUB, LANE), jnp.float32)
         for field in range(FIELDS):
@@ -178,39 +174,37 @@
                 here = (lane >= first) & (lane < first + HALO)
                 west_pack = jnp.where(here, turn(parts[0], first), west_pack)
                 east_pack = jnp.where(here, turn(parts[-1], first + HALO), east_pack)
-        pack_send[0, index] = west_pack
-        pack_send[1, index] = east_pack
-
-        return carry
-
-    assert (groups + 1) % BATCH == 0
+        pack_send[0, group] = west_pack
+        pack_send[1, group] = east_pack
+
+    assert groups % BATCH == 0
 
     def stage_batch(index, carry):
         for k in range(BATCH):
-            stage_step(index * BATCH + k, 0)
+            stage_step(index * BATCH + k)
 
         @pl.when(index == 0)
         def _():
             for side in range(2):
-                row_copy(groups, 1, side).start()
+                row_copy(0, side).start()
             for step in sideways:
                 pack_copy(0, *step).start()
-            for group in range(BATCH - 1):
+            for group in range(1, BATCH):
                 for side in range(2):
-                    row_copy(group, FIELDS, side).start()
+                    row_copy(group, side).start()
 
         return carry
 
-    lax.fori_loop(0, (groups + 1) // BATCH, stage_batch, 0)
+    lax.fori_loop(0, groups // BATCH, stage_batch, 0)
     for step in sideways:
         pack_copy(1, *step).start()
 
     def send_step(group, carry):
         for side in range(2):
-            row_copy(group, FIELDS, side).start()
+            row_copy(group, side).start()
         return carry
 
-    lax.fori_loop(BATCH - 1, groups, send_step, 0)
+    lax.fori_loop(BATCH, groups, send_step, 0)
 
     row_index = by * rows - HALO + lax.broadcasted_iota(jnp.int32, (span, LANE), 0)
     turning = 1.2 * jnp.sin(0.9 * math.pi * ((row_index.astype(jnp.float32) + 0.5) / total_rows - 0.5))
@@ -242,18 +236,18 @@
         for row in range(span):
             index = by * rows + (row - HALO)
             inside = (index >= 0) & (index < total_rows)
-            here = jnp.where(inside, jnp.broadcast_to(ext[groups, 0, row, 0:1, :], (SUB, width)), 0.0)
+            here = jnp.where(inside, jnp.broadcast_to(ext[0, 0, row, 0:1, :], (SUB, width)), 0.0)
             depth_c[row] = here
             depth_e[row] = jnp.minimum(here, east(here))
             if row > 0:
                 depth_n[row - 1] = jnp.minimum(before, here)
             before = here
             for axis in range(2):
-                wind = jnp.broadcast_to(ext[groups, 0, row, 2 + axis : 3 + axis, :], (SUB, width))
-                stress[axis, row] = jnp.where(sub == 0, WIND * wind, 0.0)
+                wind = jnp.broadcast_to(ext[0, 1, row, axis : axis + 1, :], (SUB, width))
+                stress[axis, row] = jnp.where(sub == lead, WIND * wind, 0.0)
             place = (row + span - HALO) % span
             flat[0, place : place + 1, :] = here[0:1, :]
-            flat[1, place : place + 1, :] = ext[groups, 0, row, 1:2, :]
+            flat[1, place : place + 1, :] = ext[0, 0, row, 1:2, :]
         depth = flat[0]
         ssh = flat[1]
         near = jnp.minimum(depth, east(depth))
@@ -269,11 +263,12 @@
         return jnp.where(mask, value, 0.0)
 
     def tendencies(group):
-        number = level + (group * SUB).astype(jnp.float32)
-
-        def stage_pass(part, carry):
-            slot = jnp.where(part == 0, group, groups + part)
-            after = groups + 1 + part
+        number = level + (group * SUB - lead).astype(jnp.float32)
+        number = jnp.where(number < 0.0, 1e9, number)
+
+        def stage_pass(part):
+            slot = group if part == 0 else groups
+            keep = width if part == 0 else cols
 
             def first_block(index, inner):
                 row = 1 + 2 * part + index * FIRST
@@ -309,69 +304,81 @@
 
             def second_block(index, inner):
                 row = 2 + 2 * part + index * SECOND
-                wet = [number < depth_c[row + k] for k in range(SECOND)]
+                wet = [(number < depth_c[row + k])[:, :keep] for k in range(SECOND)]
                 wet_e = [number < depth_e[row + k] for k in range(SECOND)]
-                wet_n = [number < depth_n[row - 1 + k] for k in range(SECOND + 1)]
+                wet_n = [(number < depth_n[row - 1 + k])[:, :keep] for k in range(SECOND + 1)]
+
+                def differences(cells):
+                    faces = [
+                        cut(wet_n[k], cells[k + 1][:, :keep] - cells[k][:, :keep]) for k in range(SECOND + 1)
+                    ]
+                    result = []
+                    for k in range(SECOND):
+                        here = cells[k + 1]
+                        face_e = cut(wet_e[k], east(here) - here)
+                        result.append((face_e[:, :keep], west(face_e)[:, :keep], faces[k + 1], faces[k]))
+                    return result
+
+                forced = []
                 cells = [press[part, row - 1 + k] for k in range(SECOND + 2)]
-                faces = [cut(wet_n[k], cells[k + 1] - cells[k]) for k in range(SECOND + 1)]
-                forced = []
-                for k in range(SECOND):
-                    here = cells[k + 1]
-                    face_e = cut(wet_e[k], east(here) - here)
-                    turned = jnp.concatenate([cor[row + k]] * (width // LANE), axis=1)
+                for k, (face_e, face_w, face_n, face_s) in enumerate(differences(cells)):
+                    turned = jnp.concatenate([cor[row + k]] * (keep // LANE), axis=1)
                     forced.append((
-                        cut(wet[k], turned * ext[slot, 1, row + k]) - 0.5 * (face_e + west(face_e)),
-                        cut(wet[k], -turned * ext[slot, 0, row + k]) - 0.5 * (faces[k + 1] + faces[k]),
+                        cut(wet[k], turned * ext[slot, 1, row + k, :, :keep]) - 0.5 * (face_e + face_w),
+                        cut(wet[k], -turned * ext[slot, 0, row + k, :, :keep]) - 0.5 * (face_n + face_s),
                     ))
                 results = []
                 for field in range(FIELDS):
                     cells = [lap[field, row - 1 + k] for k in range(SECOND + 2)]
-                    faces = [cut(wet_n[k], cells[k + 1] - cells[k]) for k in range(SECOND + 1)]
-                    for k in range(SECOND):
-                        here = cells[k + 1]
-                        face_e = cut(wet_e[k], east(here) - here)
-                        twice = (face_e - west(face_e)) + (faces[k + 1] - faces[k])
-                        value = (ext[slot, field, row + k] + mix[field, row + k]) - KAPPA * twice
-                        results.append((field, row + k, value + forced[k][field] if field < 2 else value))
-                for field, place, value in results:
-                    ext[after, field, place] = value
-                return inner
-
-            lax.fori_loop(0, (span - 2 - 4 * part + FIRST - 1) // FIRST, first_block, 0)
-            lax.fori_loop(0, (span - 4 - 4 * part + SECOND - 1) // SECOND, second_block, 0)
-            @pl.when(group == 0)
-            def _():
-                for row in range(2, span - 2):
-                    for axis in range(2):
-                        ext[after, axis, row] = ext[after, axis, row] + cut(number < depth_c[row], stress[axis, row])
-
-            return carry
-
-        lax.fori_loop(0, 2, stage_pass, 0)
-
-        def finish_block(index, carry):
-            for k in range(FINISH):
-                row = index * FINISH + k
-                wet = (number < depth_c[row + HALO])[:, :cols]
-                for field in range(FIELDS):
-                    value = 0.5 * (
-                        ext[group, field, row + HALO, :, :cols] + ext[groups + 2, field, row + HALO, :, :cols]
-                    )
+                    for k, (face_e, face_w, face_n, face_s) in enumerate(differences(cells)):
+                        twice = (face_e - face_w) + (face_n - face_s)
+                        value = (
+                            ext[slot, field, row + k, :, :keep] + mix[field, row + k, :, :keep]
+                        ) - KAPPA * twice
+                        if field < 2:
+                            value = value + forced[k][field]
+                        if part == 1:
+                            value = 0.5 * (ext[group, field, row + k, :, :keep] + value)
+                        results.append((field, k, value))
+                for field, k, value in results:
+                    if part == 0:
+                        ext[groups, field, row + k] = value
+                        continue
+                    inner_row = row + k - HALO
                     for tile in range(tiles):
-                        own[field, tile, pl.ds(group * block + row, SUB, stride=rows), :] = value[
+                        own[field, tile, pl.ds(group * block + inner_row, SUB, stride=rows), :] = value[
                             :, tile * LANE : (tile + 1) * LANE
                         ]
                     if field < 2:
-                        flow_sum[field, row] = flow_sum[field, row] + cut(wet, value)
-            return carry
-
-        lax.fori_loop(0, rows // FINISH, finish_block, 0)
+                        flow_sum[field, inner_row] = flow_sum[field, inner_row] + cut(wet[k], value)
+                return inner
+
+            lax.fori_loop(0, (span - 2 - 4 * part + FIRST - 1) // FIRST, first_block, 0)
+            lax.fori_loop(0, (span - 4 - 4 * part + SECOND - 1) // SECOND, second_block, 0)
+
+            @pl.when(group == 0)
+            def _():
+                for row in range(2 + 2 * part, span - 2 - 2 * part):
+                    for axis in range(2):
+                        wind = cut(number < depth_c[row], stress[axis, row])
+                        if part == 0:
+                            ext[groups, axis, row] = ext[groups, axis, row] + wind
+                            continue
+                        half = 0.5 * wind[:, :cols]
+                        flow_sum[axis, row - HALO] = flow_sum[axis, row - HALO] + half
+                        for tile in range(tiles):
+                            place = pl.ds(row - HALO, SUB, stride=rows)
+                            lanes = slice(tile * LANE, (tile + 1) * LANE)
+                            own[axis, tile, place, :] = own[axis, tile, place, :] + half[:, lanes]
+
+        stage_pass(0)
+        stage_pass(1)
 
     west_lanes = (lane & 7) < HALO
 
-    def widen(index, group, fields):
-        packs = [[pack_recv[y, x, index] for x in range(2)] for y in range(3)]
-        for field in range(fields):
+    def widen(group):
+        packs = [[pack_recv[y, x, group] for x in range(2)] for y in range(3)]
+        for field in range(FIELDS):
             shifts = (
                 HALO * 8 - slot_lane(field, 0), -slot_lane(field, rows - HALO), (HALO + rows) * 8 - slot_lane(field, 0)
             )
@@ -388,20 +395,22 @@
     for step in sideways:
         pack_copy(0, *step).wait_recv()
     for side in range(2):
-        row_copy(groups, 1, side).wait_recv()
-    widen(0, groups, 1)
+        row_copy(0, side).wait_recv()
+    widen(0)
     flat_tables()
 
     def group_step(group, carry):
-        for side in range(2):
-            row_copy(group, FIELDS, side).wait_recv()
-
-        @pl.when(group == BATCH - 1)
+        @pl.when(group == BATCH)
         def _():
             for step in sideways:
                 pack_copy(1, *step).wait_recv()
 
-        widen(group + 1, group, FIELDS)
+        @pl.when(group > 0)
+        def _():
+            for side in range(2):
+                row_copy(group, side).wait_recv()
+            widen(group)
+
         tendencies(group)
         return carry
 
@@ -480,8 +489,6 @@
     surface, residual, direction = lax.fori_loop(0, ITERS - 1, solve_step, (flat[1], residual, direction))
     surface_out[...] = (surface + direction)[:rows, :cols]
 
-    for side in range(2):
-        row_copy(groups, 1, side).wait_send()
     for step in neighbours:
         moved_copy(step).wait_send()
     for step in sideways:
@@ -490,18 +497,19 @@
 
     def drain(group, carry):
         for side in range(2):
-            row_copy(group, FIELDS, side).wait_send()
+            row_copy(group, side).wait_send()
         return carry
 
     lax.fori_loop(0, groups, drain, 0)
 
 
-def deliver(levels, fields_in, surface_in, u_out, v_out, t_out, s_out, surface_out, sems):
+def deliver(fields_in, surface_in, u_out, v_out, t_out, s_out, surface_out, sems):
     outputs = (u_out, v_out, t_out, s_out)
     count = u_out.shape[0]
+    lead = fields_in.shape[2] - count
     copies = [
         pltpu.make_async_copy(
-            fields_in.at[field, tile, pl.ds(0, count)],
+            fields_in.at[field, tile, pl.ds(lead, count)],
             outputs[field].at[:, pl.ds(tile * LANE, LANE)],
             sems.at[field, tile],
         )
@@ -525,17 +533,17 @@
     f32 = jnp.float32
     flat_shape = (levels * rows, cols)
     args = [item.reshape(flat_shape) for item in (u, v, t, s)]
-    own = jax.ShapeDtypeStruct((FIELDS, tiles, (groups + 1) * SUB * rows, LANE), f32)
+    own = jax.ShapeDtypeStruct((FIELDS, tiles, groups * SUB * rows, LANE), f32)
     done, surface = pl.pallas_call(
         functools.partial(kernel, levels, rows * by_count, by_count, bx_count),
         out_shape=[pltpu.VMEM(own.shape, f32), pltpu.VMEM(ssh.shape, f32)],
         in_specs=[pl.BlockSpec(memory_space=pltpu.HBM)] * (FIELDS + 3),
         out_specs=[pl.BlockSpec(memory_space=pltpu.VMEM)] * 2,
         scratch_shapes=[
-            pltpu.VMEM((groups + 3, FIELDS, room, SUB, width), f32),
+            pltpu.VMEM((groups + 1, FIELDS, room, SUB, width), f32),
             pltpu.VMEM((rows, cols), jnp.int32),
-            pltpu.VMEM((2, groups + 1, SUB, LANE), f32),
-            pltpu.VMEM((3, 2, groups + 1, SUB, LANE), f32),
+            pltpu.VMEM((2, groups, SUB, LANE), f32),
+            pltpu.VMEM((3, 2, groups, SUB, LANE), f32),
             pltpu.VMEM((FIELDS, room, SUB, width), f32),
             pltpu.VMEM((FIELDS, room, SUB, width), f32),
             pltpu.VMEM((2, room, SUB, width), f32),
@@ -551,8 +559,8 @@
             pltpu.VMEM((2, 2, 2, rows, LANE), f32),
             pltpu.VMEM((6, span, width), f32),
             pltpu.SemaphoreType.DMA((tiles, FIELDS + 3)),
-            pltpu.SemaphoreType.DMA((2, groups + 1)),
-            pltpu.SemaphoreType.DMA((2, groups + 1)),
+            pltpu.SemaphoreType.DMA((2, groups)),
+            pltpu.SemaphoreType.DMA((2, groups)),
             pltpu.SemaphoreType.DMA((2, 6)),
             pltpu.SemaphoreType.DMA((2, 6)),
             pltpu.SemaphoreType.DMA((8,)),
@@ -563,7 +571,7 @@
         ),
     )(*args, wind.reshape(2 * rows, cols), ssh, depth)
     outs = pl.pallas_call(
-        functools.partial(deliver, levels),
+        deliver,
         out_shape=[jax.ShapeDtypeStruct(flat_shape, f32)] * FIELDS + [jax.ShapeDtypeStruct(ssh.shape, f32)],
         in_specs=[pl.BlockSpec(memory_space=pltpu.VMEM)] * 2,
         out_specs=[pl.BlockSpec(memory_space=pltpu.HBM)] * (FIELDS + 1),

time: 53.7 us -> 51.1 us (0.952)
  Pallas kernels: 52.9 us -> 50.3 us
    pallas_call x1, Pallas kernels: 51.5 us -> 48.9 us  [body(): pl.pallas_call(functools.partial(kernel, levels, rows * by_count, by_coun...]
where the time goes in v4:
time: 51.1 us; the launch traced here: 50.9 us
  Pallas kernels  50.3 us (98%)
  between operations  0.64 us (1%)
    pallas_call x1, Pallas kernels, body(): pl.pallas_call(functools.partial(kernel, levels, rows * by_count, by_coun...  48.9 us
    pallas_call x1, Pallas kernels, body(): pl.pallas_call(deliver, out_shape=[jax.ShapeDtypeStruct(flat_shape, f32)]...  1.37 us

profile of v4, /device:TPU:1, one launch (start us, length us, event | category | flops | bytes accessed | tf_op | source)
XLA Modules:
  0.0 50.9 jit_solution(9592018593797964171)
XLA Ops:
  0.6 48.9 %shard_map.110 = (f32[4,2,512,128]{3,2,1,0:T(8,128)S(1)}, f32[8,256]{1,0:T(8,128)S(1)}) custom-call(f32[496,256]{1,0:T(8,128)} %bitcast.9, f32[496,256]{1,0:T(8,128)} %bitcast.10, f32[496,256]{1,0:T(8,128)} %bitcast.11, f32[496,256]{1,0:T(8,128)} %bitcast.12, f32[16,256]{1,0:T(8,128)} %bitcast.13, f32[8,256]{1,0:T(8,128)} %ssh_in.1, s32[8,256]{1,0:T(8,128)} %depth_in.1), custom_call_target="tpu_custom_call" | custom-call | tf_op jit(solution)/shard_map/pallas_call | solution.py:537
  49.5 1.4 %shard_map.111 = (f32[496,256]{1,0:T(8,128)}, f32[496,256]{1,0:T(8,128)}, f32[496,256]{1,0:T(8,128)}, f32[496,256]{1,0:T(8,128)}, f32[8,256]{1,0:T(8,128)}) custom-call(f32[4,2,512,128]{3,2,1,0:T(8,128)S(1)} %get-tuple-element.12.fields_in, f32[8,256]{1,0:T(8,128)S(1)} %get-tuple-element.13.surface_in), custom_call_target="tpu_custom_call" | custom-call | tf_op jit(solution)/shard_map/pallas_call | solution.py:573

commit v5 on v4

--- a/solution.py
+++ b/solution.py
@@ -91,6 +91,15 @@
     def device(step_y, step_x):
         return (lax.rem(by + step_y + by_count, by_count), lax.rem(bx + step_x + bx_count, bx_count))
 
+    has_north = by < by_count - 1
+    has_south = by > 0
+
+    def where_block(y, action):
+        if y == 0:
+            action()
+        else:
+            pl.when(has_north if y > 0 else has_south)(action)
+
     neighbours = [(y, x) for y in (-1, 0, 1) for x in (-1, 0, 1) if (y, x) != (0, 0)]
 
     def load_copies():
@@ -114,8 +123,14 @@
         copy.start()
 
     barrier = pltpu.get_barrier_semaphore()
-    for step in neighbours:
-        pl.semaphore_signal(barrier, inc=1, device_id=device(*step), device_id_type=MESH)
+    for y in (0, 1, -1):
+
+        def greet(y=y):
+            for x in (-1, 0, 1):
+                if (y, x) != (0, 0):
+                    pl.semaphore_signal(barrier, inc=1, device_id=device(y, x), device_id_type=MESH)
+
+        where_block(y, greet)
 
     lane = lax.broadcasted_iota(jnp.int32, (SUB, LANE), 1)
     for tile in range(tiles):
@@ -137,6 +152,44 @@
             device_id_type=MESH,
         )
 
+    def send_all(steps, make):
+        for y in (0, 1, -1):
+
+            def act(y=y):
+                for step in steps:
+                    if step[0] == y:
+                        make(step).start()
+
+            where_block(y, act)
+
+    def receive_all(steps, make):
+        for y in (0, 1, -1):
+
+            def act(y=y):
+                for step in steps:
+                    if step[0] == y:
+                        make(step).wait_recv()
+
+            where_block(-y, act)
+
+    def sent_all(steps, make):
+        for y in (0, 1, -1):
+
+            def act(y=y):
+                for step in steps:
+                    if step[0] == y:
+                        make(step).wait_send()
+
+            where_block(y, act)
+
+    def send_rows(group):
+        send_all(lengthways, lambda step: row_copy(group, (1 - step[0]) // 2))
+
+    def receive_rows(group):
+        receive_all(lengthways, lambda step: row_copy(group, (1 - step[0]) // 2))
+
+    lengthways = [(1, 0), (-1, 0)]
+
     batches = ((0, BATCH), (BATCH, groups - BATCH))
 
     def pack_copy(batch, y, x):
@@ -157,7 +210,7 @@
         copy.wait()
     for tile in range(tiles):
         own[0, tile, :rows, :] = depth_own[:, tile * LANE : (tile + 1) * LANE].astype(jnp.float32)
-    pl.semaphore_wait(barrier, len(neighbours))
+    pl.semaphore_wait(barrier, 2 + 3 * has_north.astype(jnp.int32) + 3 * has_south.astype(jnp.int32))
 
     def stage_step(group):
         west_pack = jnp.zeros((SUB, LANE), jnp.float32)
@@ -185,23 +238,22 @@
 
         @pl.when(index == 0)
         def _():
-            for side in range(2):
-                row_copy(0, side).start()
-            for step in sideways:
-                pack_copy(0, *step).start()
-            for group in range(1, BATCH):
-                for side in range(2):
-                    row_copy(group, side).start()
+            send_rows(0)
+            send_all(sideways, lambda step: pack_copy(0, *step))
+
+            def more(group, inner):
+                send_rows(group)
+                return inner
+
+            lax.fori_loop(1, BATCH, more, 0)
 
         return carry
 
     lax.fori_loop(0, groups // BATCH, stage_batch, 0)
-    for step in sideways:
-        pack_copy(1, *step).start()
+    send_all(sideways, lambda step: pack_copy(1, *step))
 
     def send_step(group, carry):
-        for side in range(2):
-            row_copy(group, side).start()
+        send_rows(group)
         return carry
 
     lax.fori_loop(BATCH, groups, send_step, 0)
@@ -247,7 +299,7 @@
                 stress[axis, row] = jnp.where(sub == lead, WIND * wind, 0.0)
             place = (row + span - HALO) % span
             flat[0, place : place + 1, :] = here[0:1, :]
-            flat[1, place : place + 1, :] = ext[0, 0, row, 1:2, :]
+            flat[1, place : place + 1, :] = jnp.where(inside, ext[0, 0, row, 1:2, :], 0.0)
         depth = flat[0]
         ssh = flat[1]
         near = jnp.minimum(depth, east(depth))
@@ -392,23 +444,19 @@
             for row in range(span):
                 ext[group, field, row, :, cols:width] = turn(all_rows, LANE - HALO - 8 * row)
 
-    for step in sideways:
-        pack_copy(0, *step).wait_recv()
-    for side in range(2):
-        row_copy(0, side).wait_recv()
+    receive_all(sideways, lambda step: pack_copy(0, *step))
+    receive_rows(0)
     widen(0)
     flat_tables()
 
     def group_step(group, carry):
         @pl.when(group == BATCH)
         def _():
-            for step in sideways:
-                pack_copy(1, *step).wait_recv()
+            receive_all(sideways, lambda step: pack_copy(1, *step))
 
         @pl.when(group > 0)
         def _():
-            for side in range(2):
-                row_copy(group, side).wait_recv()
+            receive_rows(group)
             widen(group)
 
         tendencies(group)
@@ -437,13 +485,14 @@
             device_id=device(y, x), device_id_type=MESH,
         )
 
-    for step in neighbours:
-        moved_copy(step).start()
-    for step in neighbours:
-        moved_copy(step).wait_recv()
+    send_all(neighbours, moved_copy)
+    receive_all(neighbours, moved_copy)
     lower = lax.broadcasted_iota(jnp.int32, (SUB, cols), 0) < HALO
     lower_tile = lax.broadcasted_iota(jnp.int32, (SUB, LANE), 0) < HALO
     right = lane < LANE // 2
+    def given(side, values):
+        return jnp.where(has_north if side == 1 else has_south, values, 0.0)
+
     transports = []
     for axis in range(2):
         near = jnp.concatenate(
@@ -454,8 +503,8 @@
         ]
         far = jnp.concatenate(
             [
-                jnp.where(lower, moved_rows[1, axis], moved_rows[0, axis]),
-                jnp.where(lower_tile, corners[1], corners[0]),
+                jnp.where(lower, given(1, moved_rows[1, axis]), given(0, moved_rows[0, axis])),
+                jnp.where(lower_tile, given(1, corners[1]), given(0, corners[0])),
             ],
             axis=1,
         )
@@ -489,24 +538,20 @@
     surface, residual, direction = lax.fori_loop(0, ITERS - 1, solve_step, (flat[1], residual, direction))
     surface_out[...] = (surface + direction)[:rows, :cols]
 
-    for step in neighbours:
-        moved_copy(step).wait_send()
-    for step in sideways:
-        for batch in range(2):
-            pack_copy(batch, *step).wait_send()
+    sent_all(neighbours, moved_copy)
+    for batch in range(2):
+        sent_all(sideways, lambda step: pack_copy(batch, *step))
 
     def drain(group, carry):
-        for side in range(2):
-            row_copy(group, side).wait_send()
+        sent_all(lengthways, lambda step: row_copy(group, (1 - step[0]) // 2))
         return carry
 
     lax.fori_loop(0, groups, drain, 0)
 
 
-def deliver(fields_in, surface_in, u_out, v_out, t_out, s_out, surface_out, sems):
+def deliver(lead, fields_in, surface_in, u_out, v_out, t_out, s_out, surface_out, sems):
     outputs = (u_out, v_out, t_out, s_out)
     count = u_out.shape[0]
-    lead = fields_in.shape[2] - count
     copies = [
         pltpu.make_async_copy(
             fields_in.at[field, tile, pl.ds(lead, count)],
@@ -533,7 +578,7 @@
     f32 = jnp.float32
     flat_shape = (levels * rows, cols)
     args = [item.reshape(flat_shape) for item in (u, v, t, s)]
-    own = jax.ShapeDtypeStruct((FIELDS, tiles, groups * SUB * rows, LANE), f32)
+    own = jax.ShapeDtypeStruct((FIELDS, tiles, (groups + 1) * SUB * rows, LANE), f32)
     done, surface = pl.pallas_call(
         functools.partial(kernel, levels, rows * by_count, by_count, bx_count),
         out_shape=[pltpu.VMEM(own.shape, f32), pltpu.VMEM(ssh.shape, f32)],
@@ -571,7 +616,7 @@
         ),
     )(*args, wind.reshape(2 * rows, cols), ssh, depth)
     outs = pl.pallas_call(
-        deliver,
+        functools.partial(deliver, (groups * SUB - levels) * rows),
         out_shape=[jax.ShapeDtypeStruct(flat_shape, f32)] * FIELDS + [jax.ShapeDtypeStruct(ssh.shape, f32)],
         in_specs=[pl.BlockSpec(memory_space=pltpu.VMEM)] * 2,
         out_specs=[pl.BlockSpec(memory_space=pltpu.HBM)] * (FIELDS + 1),

time: 51.1 us -> 48.3 us (0.945)
  the two profiles are of different devices: /device:TPU:1 before, /device:TPU:6 now
where the time goes in v5:
time: 48.3 us; the launch traced here: 48.2 us
  Pallas kernels  47.6 us (99%)
  between operations  0.64 us (1%)
    pallas_call x1, Pallas kernels, body(): pl.pallas_call(functools.partial(kernel, levels, rows * by_count, by_coun...  46.2 us
    pallas_call x1, Pallas kernels, body(): pl.pallas_call(functools.partial(deliver, (groups * SUB - levels) * rows)...  1.37 us

profile of v5, /device:TPU:6, one launch (start us, length us, event | category | flops | bytes accessed | tf_op | source)
XLA Modules:
  0.0 48.2 jit_solution(557158412701944699)
XLA Ops:
  0.6 46.2 %shard_map.110 = (f32[4,2,576,128]{3,2,1,0:T(8,128)S(1)}, f32[8,256]{1,0:T(8,128)S(1)}) custom-call(f32[496,256]{1,0:T(8,128)} %bitcast.9, f32[496,256]{1,0:T(8,128)} %bitcast.10, f32[496,256]{1,0:T(8,128)} %bitcast.11, f32[496,256]{1,0:T(8,128)} %bitcast.12, f32[16,256]{1,0:T(8,128)} %bitcast.13, f32[8,256]{1,0:T(8,128)} %ssh_in.1, s32[8,256]{1,0:T(8,128)} %depth_in.1), custom_call_target="tpu_custom_call" | custom-call | tf_op jit(solution)/shard_map/pallas_call | solution.py:582
  46.8 1.4 %shard_map.111 = (f32[496,256]{1,0:T(8,128)}, f32[496,256]{1,0:T(8,128)}, f32[496,256]{1,0:T(8,128)}, f32[496,256]{1,0:T(8,128)}, f32[8,256]{1,0:T(8,128)}) custom-call(f32[4,2,576,128]{3,2,1,0:T(8,128)S(1)} %get-tuple-element.12.fields_in, f32[8,256]{1,0:T(8,128)S(1)} %get-tuple-element.13.surface_in), custom_call_target="tpu_custom_call" | custom-call | tf_op jit(solution)/shard_map/pallas_call | solution.py:618

commit v6 on v5

--- a/solution.py
+++ b/solution.py
@@ -70,7 +70,7 @@
     levels, total_rows, by_count, bx_count,
     u_in, v_in, t_in, s_in, wind_in, ssh_in, depth_in,
     own, surface_out,
-    ext, depth_own, pack_send, pack_recv,
+    ext, depth_own, pack_send, pack_recv, far_send, far_recv,
     lap, mix, press, depth_c, depth_e, depth_n, stress, cor,
     flow_sum, moved, moved_rows, moved_cols, moved_corners, flat,
     in_sem, row_send, row_recv, pack_ss, pack_rs, moved_ss, moved_rs,
@@ -195,9 +195,15 @@
     def pack_copy(batch, y, x):
         first, count = batches[batch]
         place = 2 * (y % 3) + (1 - x) // 2
+        if y == 0:
+            source = pack_send.at[(1 + x) // 2, pl.ds(first, count)]
+            target = pack_recv.at[(1 - x) // 2, pl.ds(first, count)]
+        else:
+            source = far_send.at[(1 - y) // 2, (1 + x) // 2, pl.ds(first // 2, count // 2)]
+            target = far_recv.at[(1 - y) // 2, (1 - x) // 2, pl.ds(first // 2, count // 2)]
         return pltpu.make_async_remote_copy(
-            src_ref=pack_send.at[(1 + x) // 2, pl.ds(first, count)],
-            dst_ref=pack_recv.at[y % 3, (1 - x) // 2, pl.ds(first, count)],
+            src_ref=source,
+            dst_ref=target,
             send_sem=pack_ss.at[batch, place],
             recv_sem=pack_rs.at[batch, place],
             device_id=device(y, x),
@@ -229,12 +235,18 @@
                 east_pack = jnp.where(here, turn(parts[-1], first + HALO), east_pack)
         pack_send[0, group] = west_pack
         pack_send[1, group] = east_pack
-
-    assert groups % BATCH == 0
+        return west_pack, east_pack
+
+    assert groups % BATCH == 0 and BATCH % 2 == 0
+    upper = (lane & 32) != 0
 
     def stage_batch(index, carry):
-        for k in range(BATCH):
-            stage_step(index * BATCH + k)
+        for k in range(BATCH // 2):
+            pair = index * (BATCH // 2) + k
+            packs = stage_step(2 * pair), stage_step(2 * pair + 1)
+            for side in range(2):
+                far_send[0, side, pair] = jnp.where(upper, packs[0][side], turn(packs[1][side], -32))
+                far_send[1, side, pair] = jnp.where(upper, turn(packs[1][side], 32), packs[0][side])
 
         @pl.when(index == 0)
         def _():
@@ -429,7 +441,13 @@
     west_lanes = (lane & 7) < HALO
 
     def widen(group):
-        packs = [[pack_recv[y, x, group] for x in range(2)] for y in range(3)]
+        pair = lax.div(jnp.int32(group), jnp.int32(2))
+        odd = lax.rem(jnp.int32(group), jnp.int32(2))
+        packs = [
+            [pack_recv[x, group] for x in range(2)],
+            [pltpu.roll(far_recv[0, x, pair], 32 * odd, 1) for x in range(2)],
+            [pltpu.roll(far_recv[1, x, pair], 96 * odd, 1) for x in range(2)],
+        ]
         for field in range(FIELDS):
             shifts = (
                 HALO * 8 - slot_lane(field, 0), -slot_lane(field, rows - HALO), (HALO + rows) * 8 - slot_lane(field, 0)
@@ -588,7 +606,9 @@
             pltpu.VMEM((groups + 1, FIELDS, room, SUB, width), f32),
             pltpu.VMEM((rows, cols), jnp.int32),
             pltpu.VMEM((2, groups, SUB, LANE), f32),
-            pltpu.VMEM((3, 2, groups, SUB, LANE), f32),
+            pltpu.VMEM((2, groups, SUB, LANE), f32),
+            pltpu.VMEM((2, 2, groups // 2, SUB, LANE), f32),
+            pltpu.VMEM((2, 2, groups // 2, SUB, LANE), f32),
             pltpu.VMEM((FIELDS, room, SUB, width), f32),
             pltpu.VMEM((FIELDS, room, SUB, width), f32),
             pltpu.VMEM((2, room, SUB, width), f32),

time: 48.3 us -> 47.9 us (level); the launches traced: 48.2 us -> 47.3 us
  Pallas kernels: 47.6 us -> 46.7 us
    pallas_call x1, Pallas kernels: 46.2 us -> 45.3 us  [body(): pl.pallas_call(functools.partial(kernel, levels, rows * by_count, by_coun...]
where the time goes in v6:
time: 47.9 us; the launch traced here: 47.3 us
  Pallas kernels  46.7 us (97%)
  between operations  0.64 us (1%)
    pallas_call x1, Pallas kernels, body(): pl.pallas_call(functools.partial(kernel, levels, rows * by_count, by_coun...  45.3 us
    pallas_call x1, Pallas kernels, body(): pl.pallas_call(functools.partial(deliver, (groups * SUB - levels) * rows)...  1.37 us

profile of v6, /device:TPU:6, one launch (start us, length us, event | category | flops | bytes accessed | tf_op | source)
XLA Modules:
  0.0 47.3 jit_solution(18387262461680533704)
XLA Ops:
  0.6 45.3 %shard_map.110 = (f32[4,2,576,128]{3,2,1,0:T(8,128)S(1)}, f32[8,256]{1,0:T(8,128)S(1)}) custom-call(f32[496,256]{1,0:T(8,128)} %bitcast.9, f32[496,256]{1,0:T(8,128)} %bitcast.10, f32[496,256]{1,0:T(8,128)} %bitcast.11, f32[496,256]{1,0:T(8,128)} %bitcast.12, f32[16,256]{1,0:T(8,128)} %bitcast.13, f32[8,256]{1,0:T(8,128)} %ssh_in.1, s32[8,256]{1,0:T(8,128)} %depth_in.1), custom_call_target="tpu_custom_call" | custom-call | tf_op jit(solution)/shard_map/pallas_call | solution.py:600
  45.9 1.4 %shard_map.111 = (f32[496,256]{1,0:T(8,128)}, f32[496,256]{1,0:T(8,128)}, f32[496,256]{1,0:T(8,128)}, f32[496,256]{1,0:T(8,128)}, f32[8,256]{1,0:T(8,128)}) custom-call(f32[4,2,576,128]{3,2,1,0:T(8,128)S(1)} %get-tuple-element.12.fields_in, f32[8,256]{1,0:T(8,128)S(1)} %get-tuple-element.13.surface_in), custom_call_target="tpu_custom_call" | custom-call | tf_op jit(solution)/shard_map/pallas_call | solution.py:638

commit v7 on v6

--- a/solution.py
+++ b/solution.py
@@ -23,7 +23,7 @@
 HALO = 4
 SUB = 8
 LANE = 128
-BATCH = 4
+BATCH = 2
 FIRST = 5
 SECOND = 4
 
@@ -102,14 +102,22 @@
 
     neighbours = [(y, x) for y in (-1, 0, 1) for x in (-1, 0, 1) if (y, x) != (0, 0)]
 
-    def load_copies():
+    def load_copies(late):
         result = []
+        start = BATCH * block if late else lead * rows
+        count = (groups - BATCH) * block if late else BATCH * block - lead * rows
         for tile in range(tiles):
             lanes = pl.ds(tile * LANE, LANE)
             for field in range(FIELDS):
                 result.append(pltpu.make_async_copy(
-                    inputs[field].at[:, lanes], own.at[field, tile, pl.ds(lead * rows, levels * rows)], in_sem.at[tile, field]
+                    inputs[field].at[pl.ds(start - lead * rows, count), lanes],
+                    own.at[field, tile, pl.ds(start, count)],
+                    in_sem.at[tile + tiles * late, field],
                 ))
+        if late:
+            return result
+        for tile in range(tiles):
+            lanes = pl.ds(tile * LANE, LANE)
             result.append(pltpu.make_async_copy(
                 ssh_in.at[:, lanes], own.at[0, tile, pl.ds(rows, rows)], in_sem.at[tile, FIELDS]
             ))
@@ -119,7 +127,7 @@
         result.append(pltpu.make_async_copy(depth_in, depth_own, in_sem.at[0, FIELDS + 2]))
         return result
 
-    for copy in load_copies():
+    for copy in load_copies(0) + load_copies(1):
         copy.start()
 
     barrier = pltpu.get_barrier_semaphore()
@@ -153,7 +161,7 @@
         )
 
     def send_all(steps, make):
-        for y in (0, 1, -1):
+        for y in (1, -1, 0):
 
             def act(y=y):
                 for step in steps:
@@ -212,7 +220,7 @@
 
     sideways = [(y, x) for y in (0, 1, -1) for x in (-1, 1)]
 
-    for copy in load_copies():
+    for copy in load_copies(0):
         copy.wait()
     for tile in range(tiles):
         own[0, tile, :rows, :] = depth_own[:, tile * LANE : (tile + 1) * LANE].astype(jnp.float32)
@@ -258,6 +266,8 @@
                 return inner
 
             lax.fori_loop(1, BATCH, more, 0)
+            for copy in load_copies(1):
+                copy.wait()
 
         return carry
 
@@ -340,7 +350,7 @@
                 wet_e = [number < depth_e[row + k] for k in range(FIRST)]
                 wet_n = [number < depth_n[row - 1 + k] for k in range(FIRST + 1)]
                 speed = [
-                    [(-0.5 * ADVECT) * ext[slot, field, row + k] for field in range(2)] for k in range(FIRST)
+                    [(-0.5 * ADVECT) * ext[slot, field, row + k, :, :keep] for field in range(2)] for k in range(FIRST)
                 ]
                 for field in range(FIELDS):
                     cells = [ext[slot, field, row - 1 + k] for k in range(FIRST + 2)]
@@ -350,9 +360,9 @@
                         face_e = cut(wet_e[k], east(here) - here)
                         face_w = west(face_e)
                         lap[field, row + k] = (face_e - face_w) + (faces[k + 1] - faces[k])
-                        mix[field, row + k] = speed[k][0] * (face_e + face_w) + speed[k][1] * (
-                            faces[k + 1] + faces[k]
-                        )
+                        along_x = (face_e + face_w)[:, :keep]
+                        along_y = (faces[k + 1] + faces[k])[:, :keep]
+                        mix[field, row + k, :, :keep] = speed[k][0] * along_x + speed[k][1] * along_y
                 above = [
                     jnp.broadcast_to(press[part, row + k, SUB - 1 : SUB, :], (SUB, width)) for k in range(FIRST)
                 ]
@@ -623,7 +633,7 @@
             pltpu.VMEM((2, 2, rows, LANE), f32),
             pltpu.VMEM((2, 2, 2, rows, LANE), f32),
             pltpu.VMEM((6, span, width), f32),
-            pltpu.SemaphoreType.DMA((tiles, FIELDS + 3)),
+            pltpu.SemaphoreType.DMA((2 * tiles, FIELDS + 3)),
             pltpu.SemaphoreType.DMA((2, groups)),
             pltpu.SemaphoreType.DMA((2, groups)),
             pltpu.SemaphoreType.DMA((2, 6)),

time: 47.9 us -> 47.8 us (level)
  no operation moved by 1% of the time
where the time goes in v7:
time: 47.8 us; the launch traced here: 47.2 us
  Pallas kernels  46.6 us (97%)
  between operations  0.64 us (1%)
    pallas_call x1, Pallas kernels, body(): pl.pallas_call(functools.partial(kernel, levels, rows * by_count, by_coun...  45.2 us
    pallas_call x1, Pallas kernels, body(): pl.pallas_call(functools.partial(deliver, (groups * SUB - levels) * rows)...  1.37 us

profile of v7, /device:TPU:6, one launch (start us, length us, event | category | flops | bytes accessed | tf_op | source)
XLA Modules:
  0.0 47.2 jit_solution(5714210758979351235)
XLA Ops:
  0.6 45.2 %shard_map.110 = (f32[4,2,576,128]{3,2,1,0:T(8,128)S(1)}, f32[8,256]{1,0:T(8,128)S(1)}) custom-call(f32[496,256]{1,0:T(8,128)} %bitcast.9, f32[496,256]{1,0:T(8,128)} %bitcast.10, f32[496,256]{1,0:T(8,128)} %bitcast.11, f32[496,256]{1,0:T(8,128)} %bitcast.12, f32[16,256]{1,0:T(8,128)} %bitcast.13, f32[8,256]{1,0:T(8,128)} %ssh_in.1, s32[8,256]{1,0:T(8,128)} %depth_in.1), custom_call_target="tpu_custom_call" | custom-call | tf_op jit(solution)/shard_map/pallas_call | solution.py:610
  45.8 1.4 %shard_map.111 = (f32[496,256]{1,0:T(8,128)}, f32[496,256]{1,0:T(8,128)}, f32[496,256]{1,0:T(8,128)}, f32[496,256]{1,0:T(8,128)}, f32[8,256]{1,0:T(8,128)}) custom-call(f32[4,2,576,128]{3,2,1,0:T(8,128)S(1)} %get-tuple-element.12.fields_in, f32[8,256]{1,0:T(8,128)S(1)} %get-tuple-element.13.surface_in), custom_call_target="tpu_custom_call" | custom-call | tf_op jit(solution)/shard_map/pallas_call | solution.py:648
